TPU v7x, 32 devices: a whole 2x2x4 slice. The times are simulated.
32 devices in a mesh: rep: 8 (over y, x, core), shard: 4 (over z).
Axes of the slice: x: 2, y: 2, z: 4, core: 2. Of those that a mesh axis runs over, the one named last changes fastest.
Arguments:
- tokens: bfloat16 [16384, 1024], P(('rep', 'shard')), may hold values from -6 to 6
- cotangent: bfloat16 [16384, 1024], P(('rep', 'shard')), may hold values from -6 to 6
- seq_lengths: int32 [8, 4], P('rep'), may hold values from 1 to 1536, as said below
- qkv_weight: float32 [1024, 3072], P('shard'), may hold values from -0.1875 to 0.1875
- out_weight: float32 [1024, 1024], P('shard'), may hold values from -0.75 to 0.75
- up_weight: float32 [1024, 4096], P('shard'), may hold values from -0.1875 to 0.1875
- down_weight: float32 [4096, 1024], P('shard'), may hold values from -0.09375 to 0.09375
- vectors: float32 [12288], replicated, may hold values from -0.9 to 2.25
- row_state: float32 [3, 1024], P(None, 'shard'), may hold values from 137.6256 to 12451.84, as said below
- down_rows: float32 [4096], P('shard'), may hold values from 137.6256 to 12451.84, as said below
- col_state: float32 [9216], replicated, may hold values from 137.6256 to 12451.84, as said below
- vector_state: float32 [12288], replicated, may hold values from 1474.56 to 6225.92
Outputs:
- block_out: bfloat16 [16384, 1024], P(('rep', 'shard'))
- tokens_grad: bfloat16 [16384, 1024], P(('rep', 'shard'))
- qkv_grad: float32 [1024, 3072], P('shard')
- out_grad: float32 [1024, 1024], P('shard')
- up_grad: float32 [1024, 4096], P('shard')
- down_grad: float32 [4096, 1024], P('shard')
- vector_grad: float32 [12288], replicated
- qkv_new: float32 [1024, 3072], P('shard')
- out_new: float32 [1024, 1024], P('shard')
- up_new: float32 [1024, 4096], P('shard')
- down_new: float32 [4096, 1024], P('shard')
- vector_new: float32 [12288], replicated
- qkv_copy: bfloat16 [1024, 3072], P('shard')
- out_copy: bfloat16 [1024, 1024], P('shard')
- up_copy: bfloat16 [1024, 4096], P('shard')
- down_copy: bfloat16 [4096, 1024], P('shard')
- row_state_new: float32 [3, 1024], P(None, 'shard')
- down_rows_new: float32 [4096], P('shard')
- col_state_new: float32 [9216], replicated
- vector_state_new: float32 [12288], replicated
- update_rms: float32 [5], replicated
Inputs may be any that keep to these rules, and one draw needn't show every extreme that they name: `seq_lengths`: in every group one sequence, never the first or the last, has exactly 1536 tokens; the other 3 have together 512 tokens. `row_state`: every entry is positive. `down_rows`: every entry is positive. `col_state`: every entry is positive.
All inputs are finite; a program needn't handle non-finite values.
Results may differ from a plain program's by a relative error of at most 0.013.
Values may be sent and summed in bfloat16 or wider, within the bound.
No kernel may reach another device: no remote copies, remote signals or barrier semaphores. Data moves between devices by JAX's collectives and lax.ppermute only.
A program may use at most 320 MiB of HBM per device.

v0:
```python
import functools

import jax
import jax.numpy as jnp
from jax import lax
from jax.experimental import pallas as pl
from jax.experimental.pallas import tpu as pltpu
from jax.sharding import PartitionSpec as P

HEADS = 16
STEP = 10
BLOCK = 256


eps_norm = 1e-05
eps_second = 1e-30
rate_step = 0.5
clip_level = 1.0
masked = -1e30
gelu_root = (2.0 / 3.141592653589793) ** 0.5
gelu_cubic = 0.044715

f32 = jnp.float32
bf16 = jnp.bfloat16


def norm_parts(values):
    average = jnp.mean(values, axis=-1, keepdims=True)
    centred = values - average
    inv_std = lax.rsqrt(jnp.mean(centred * centred, axis=-1, keepdims=True) + eps_norm)
    return (centred * inv_std, inv_std)


def norm_back(grad_out, normed, inv_std, gain_vec):
    grad_normed = grad_out * gain_vec
    inner_mean = jnp.mean(grad_normed * normed, axis=-1, keepdims=True)
    centred = grad_normed - jnp.mean(grad_normed, axis=-1, keepdims=True)
    return (centred - normed * inner_mean) * inv_std


def gelu_value(pre_act):
    curve = jnp.tanh(gelu_root * (pre_act + gelu_cubic * pre_act * pre_act * pre_act))
    return 0.5 * pre_act * (1.0 + curve)


def gelu_slope(pre_act):
    square = pre_act * pre_act
    curve = jnp.tanh(gelu_root * (pre_act + gelu_cubic * square * pre_act))
    inner = gelu_root * (1.0 + 3.0 * gelu_cubic * square)
    return 0.5 * (1.0 + curve) + 0.5 * pre_act * (1.0 - curve * curve) * inner


def dot(left_side, right_side):
    return jnp.dot(left_side, right_side, preferred_element_type=f32)


def dot_right(left_side, right_side):
    return lax.dot_general(
        left_side, right_side, (((1,), (1,)), ((), ())), preferred_element_type=f32
    )


def dot_rows(left_side, right_side):
    return lax.dot_general(
        left_side, right_side, (((0,), (0,)), ((), ())), preferred_element_type=f32
    )


def pick(stack, index, axis=0):
    return lax.dynamic_index_in_dim(stack, index, axis, keepdims=False, allow_negative_indices=False)


def cut_rows(values, start, count):
    return lax.dynamic_slice_in_dim(values, start, count, 0, allow_negative_indices=False)


def place(stack, part, index, axis=0):
    return lax.dynamic_update_index_in_dim(stack, part, index, axis, allow_negative_indices=False)


def head_rows(number, head_width):
    return slice(number * head_width, (number + 1) * head_width)


def lane_masks(block_rows, width, heads):
    lanes = lax.broadcasted_iota(jnp.int32, (block_rows, width), 1)
    head_width = width // heads
    return [
        (lanes >= number * head_width) & (lanes < (number + 1) * head_width)
        for number in range(heads)
    ]


def allowed_pairs(key_block, query_block, start_row, block):
    key_pos = lax.broadcasted_iota(jnp.int32, (block, block), 0) + key_block * block
    query_pos = lax.broadcasted_iota(jnp.int32, (block, block), 1) + query_block * block
    return (key_pos <= query_pos) & (key_pos >= start_row)


def key_offsets(key_block, query_block, block):
    rows = lax.broadcasted_iota(jnp.int32, (block, 1), 0)
    return (rows + (key_block - query_block) * block).astype(f32)


def turned(values):
    return jnp.transpose(values.astype(f32))


def head_stack(values, lanes):
    zero = jnp.zeros(values.shape, values.dtype)
    return jnp.concatenate([jnp.where(lane, values, zero) for lane in lanes], axis=0)


def eights(values, combine):
    rows, columns = values.shape
    return combine(values.reshape(rows // 8, 8, columns), axis=0)


def forward_kernel(
    heads,
    block,
    low_ref,
    mid_ref,
    slope_ref,
    start_ref,
    qkv_ref,
    out_ref,
    log_ref,
    values_turned,
    key_stack,
    score_ref,
):
    tokens = qkv_ref.shape[0]
    width = qkv_ref.shape[1] // 3
    head_width = width // heads
    blocks = tokens // block
    query_block = pl.program_id(0)

    @pl.when(query_block == 0)
    def _():
        lanes = lane_masks(block, width, heads)
        for number in range(blocks):
            rows = slice(number * block, (number + 1) * block)
            values_turned[number] = turned(qkv_ref[rows, 2 * width :]).astype(bf16)
            key_stack[number] = head_stack(qkv_ref[rows, width : 2 * width], lanes)

    first_row = pl.multiple_of(query_block * block, block)
    queries = qkv_ref[pl.ds(first_row, block), :width].astype(f32) * head_width ** (-0.5)
    queries = turned(queries).astype(bf16)
    start_row = start_ref[query_block]

    def score_step(key_block, bests, with_mask):
        scores = dot(key_stack[key_block], queries)
        offsets = key_offsets(key_block, query_block, block)
        allowed = allowed_pairs(key_block, query_block, start_row, block) if with_mask else None
        result = []
        for number in range(heads):
            rows = head_rows(number, block)
            part = scores[rows] + slope_ref[number] * offsets
            if with_mask:
                part = jnp.where(allowed, part, masked)
            score_ref[key_block, rows, :] = part
            result.append(jnp.maximum(bests[number], eights(part, jnp.max)))
        return tuple(result)

    low, mid = low_ref[query_block], mid_ref[query_block]
    bests = tuple(jnp.full((8, block), masked, f32) for _ in range(heads))
    bests = lax.fori_loop(low, mid, functools.partial(score_step, with_mask=True), bests)
    bests = lax.fori_loop(mid, query_block, functools.partial(score_step, with_mask=False), bests)
    bests = score_step(query_block, bests, True)
    bests = [jnp.max(best, axis=0, keepdims=True) for best in bests]

    def value_step(key_block, state):
        result = []
        for number in range(heads):
            total, gathered = state[2 * number : 2 * number + 2]
            weights = jnp.exp(score_ref[key_block, head_rows(number, block), :] - bests[number])
            value_rows = values_turned[key_block, head_rows(number, head_width), :]
            result += [
                total + eights(weights, jnp.sum),
                gathered + dot(value_rows, weights.astype(bf16)),
            ]
        return tuple(result)

    state = ()
    for number in range(heads):
        state += (jnp.zeros((8, block), f32), jnp.zeros((head_width, block), f32))
    state = lax.fori_loop(low, query_block + 1, value_step, state)
    columns = []
    for number in range(heads):
        total = jnp.sum(state[2 * number], axis=0, keepdims=True)
        columns.append(state[2 * number + 1] / total)
        log_ref[0, number : number + 1, :] = bests[number] + jnp.log(total)
    out_ref[...] = jnp.transpose(jnp.concatenate(columns, axis=0)).astype(bf16)


def backward_kernel(heads, block, first_head, merge, *refs):
    full_ref, high_ref, slope_ref, start_ref, log_ref, qkv_ref, grad_ref, out_ref = refs[:8]
    earlier_ref = refs[8] if merge else None
    result_ref = refs[9 if merge else 8]
    (
        queries_turned,
        grads_turned,
        keys_turned,
        query_stack,
        grad_stack,
        key_stack,
        value_stack,
        delta_rows,
        query_grads,
    ) = refs[10 if merge else 9 :]
    tokens, all_width = grad_ref.shape
    head_width = all_width // log_ref.shape[1]
    width = heads * head_width
    scale = head_width ** (-0.5)
    blocks = tokens // block
    key_block = pl.program_id(0)
    lanes = lane_masks(block, width, heads)

    def columns(kind):
        start = kind * all_width + first_head * head_width
        return slice(start, start + width)

    def target(kind):
        start = (kind * all_width + first_head * head_width) if merge else kind * width
        return slice(start, start + width)

    @pl.when(key_block == 0)
    def _():
        for number in range(blocks):
            rows = slice(number * block, (number + 1) * block)
            queries = qkv_ref[rows, columns(0)]
            queries_turned[number] = turned(queries.astype(f32) * scale).astype(bf16)
            query_stack[number] = head_stack(queries, lanes)
            keys_turned[number] = turned(qkv_ref[rows, columns(1)]).astype(bf16)
            grads = grad_ref[rows, columns(0)]
            grad_stack[number] = head_stack(grads, lanes)
            grads = grads.astype(f32)
            grads_turned[number] = turned(grads).astype(bf16)
            product = turned(grads * out_ref[rows, columns(0)].astype(f32))
            for head in range(heads):
                delta_rows[number, head : head + 1, :] = jnp.sum(
                    product[head_rows(head, head_width)], axis=0, keepdims=True
                )
            query_grads[number] = jnp.zeros((width, block), f32)

    key_row = pl.multiple_of(key_block * block, block)
    key_stack[...] = head_stack(qkv_ref[pl.ds(key_row, block), columns(1)], lanes)
    value_stack[...] = head_stack(qkv_ref[pl.ds(key_row, block), columns(2)], lanes)

    def step(query_block, state, with_mask):
        key_total, value_total = state
        scores = dot(key_stack[...], queries_turned[query_block])
        grad_weights = dot(value_stack[...], grads_turned[query_block])
        offsets = key_offsets(key_block, query_block, block)
        if with_mask:
            allowed = allowed_pairs(key_block, query_block, start_ref[query_block], block)
        weight_list, grad_list = [], []
        for number in range(heads):
            rows = head_rows(number, block)
            head = first_head + number
            part = scores[rows] + slope_ref[head] * offsets
            part = part - log_ref[query_block, head : head + 1, :]
            if with_mask:
                part = jnp.where(allowed, part, masked)
            probabilities = jnp.exp(part)
            delta = delta_rows[query_block, number : number + 1, :]
            grad_scores = (probabilities * (grad_weights[rows] - delta)).astype(bf16)
            weight_list.append(probabilities.astype(bf16))
            grad_list.append(grad_scores)
            rows = head_rows(number, head_width)
            query_grads[query_block, rows, :] += dot(keys_turned[key_block, rows, :], grad_scores)
        weight_row = jnp.concatenate(weight_list, axis=1)
        grad_row = jnp.concatenate(grad_list, axis=1)
        return (
            key_total + dot(grad_row, query_stack[query_block]),
            value_total + dot(weight_row, grad_stack[query_block]),
        )

    state = (jnp.zeros((block, width), f32), jnp.zeros((block, width), f32))
    state = step(key_block, state, True)
    full, high = full_ref[key_block], high_ref[key_block]
    state = lax.fori_loop(key_block + 1, full, functools.partial(step, with_mask=False), state)
    state = lax.fori_loop(full, high, functools.partial(step, with_mask=True), state)
    result_ref[pl.ds(key_row, block), target(1)] = (state[0] * scale).astype(bf16)
    result_ref[pl.ds(key_row, block), target(2)] = state[1].astype(bf16)
    if merge:
        other = first_head * head_width
        for kind in range(3):
            result_ref[pl.ds(key_row, block), kind * all_width : kind * all_width + other] = earlier_ref[
                pl.ds(key_row, block), kind * other : (kind + 1) * other
            ]

    @pl.when(key_block == blocks - 1)
    def _():
        for number in range(blocks):
            rows = slice(number * block, (number + 1) * block)
            result_ref[rows, target(0)] = jnp.transpose(query_grads[number] * scale).astype(bf16)


def block_plan(lengths, tokens, block):
    ends = jnp.cumsum(lengths)
    positions = jnp.arange(tokens, dtype=jnp.int32)
    passed = positions[:, None] >= ends[None, :]
    starts = jnp.max(jnp.where(passed, ends[None, :], 0), axis=1).astype(jnp.int32)
    finish = jnp.min(jnp.where(passed, tokens, ends[None, :]), axis=1).astype(jnp.int32)
    blocks = tokens // block
    number = jnp.arange(blocks, dtype=jnp.int32)
    first_start = starts[::block]
    last_start = starts[block - 1 :: block]
    low = first_start // block
    mid = jnp.clip((last_start + block - 1) // block, low, number)
    high = (finish[block - 1 :: block] - 1) // block + 1
    full = jnp.clip(finish[::block] // block, number + 1, high)
    return (starts.reshape(blocks, 1, block), low, mid, full, high)


def scalar_spec():
    return pl.BlockSpec(memory_space=pltpu.SMEM)


def whole_spec(shape):
    return pl.BlockSpec(shape, lambda step: (0,) * len(shape), pipeline_mode=pl.Buffered(1))


def attend_forward(qkv, plan, slopes, heads, block):
    tokens, triple = qkv.shape
    width = triple // 3
    blocks = tokens // block
    starts, low, mid, full, high = plan
    return pl.pallas_call(
        functools.partial(forward_kernel, heads, block),
        grid=(blocks,),
        in_specs=[
            scalar_spec(),
            scalar_spec(),
            scalar_spec(),
            whole_spec((blocks, 1, block)),
            whole_spec((tokens, triple)),
        ],
        out_specs=[
            pl.BlockSpec((block, width), lambda step: (step, 0)),
            pl.BlockSpec((1, heads, block), lambda step: (step, 0, 0)),
        ],
        out_shape=[
            jax.ShapeDtypeStruct((tokens, width), bf16),
            jax.ShapeDtypeStruct((blocks, heads, block), f32),
        ],
        scratch_shapes=[
            pltpu.VMEM((blocks, width, block), bf16),
            pltpu.VMEM((blocks, heads * block, width), bf16),
            pltpu.VMEM((blocks, heads * block, block), f32),
        ],
        compiler_params=pltpu.CompilerParams(
            dimension_semantics=("arbitrary",), vmem_limit_bytes=24 * 1024 * 1024
        ),
        cost_estimate=pl.CostEstimate(
            flops=3 * tokens * tokens * 256 * heads,
            bytes_accessed=10 * tokens * width,
            transcendentals=tokens * tokens * heads // 2,
        ),
        name="attend_forward",
    )(low, mid, slopes, starts, qkv)


def attend_backward(qkv, grads, outputs, logs, plan, slopes, heads, block, first_head, earlier):
    tokens, triple = qkv.shape
    all_width = triple // 3
    all_heads = logs.shape[1]
    width = all_width // all_heads * heads
    blocks = tokens // block
    starts, low, mid, full, high = plan
    merge = earlier is not None
    result_width = triple if merge else 3 * width
    operands = [full, high, slopes, starts, logs, qkv, grads, outputs]
    specs = [scalar_spec() for _ in range(3)] + [whole_spec(entry.shape) for entry in operands[3:]]
    if merge:
        operands.append(earlier)
        specs.append(whole_spec(earlier.shape))
    return pl.pallas_call(
        functools.partial(backward_kernel, heads, block, first_head, merge),
        grid=(blocks,),
        in_specs=specs,
        out_specs=pl.BlockSpec((tokens, result_width), lambda step: (0, 0)),
        out_shape=jax.ShapeDtypeStruct((tokens, result_width), bf16),
        scratch_shapes=[
            pltpu.VMEM((blocks, width, block), bf16),
            pltpu.VMEM((blocks, width, block), bf16),
            pltpu.VMEM((blocks, width, block), bf16),
            pltpu.VMEM((blocks, heads * block, width), bf16),
            pltpu.VMEM((blocks, heads * block, width), bf16),
            pltpu.VMEM((heads * block, width), bf16),
            pltpu.VMEM((heads * block, width), bf16),
            pltpu.VMEM((blocks, heads, block), f32),
            pltpu.VMEM((blocks, width, block), f32),
        ],
        compiler_params=pltpu.CompilerParams(
            dimension_semantics=("arbitrary",), vmem_limit_bytes=24 * 1024 * 1024
        ),
        cost_estimate=pl.CostEstimate(
            flops=8 * tokens * tokens * 256 * heads,
            bytes_accessed=20 * tokens * width,
            transcendentals=tokens * tokens * heads // 2,
        ),
        name="attend_backward",
    )(*operands)


def hidden_backward_kernel(own_ref, other_ref, weight_ref, slope_ref, result_ref, total_ref):
    rows = own_ref.shape[0]
    total = jnp.zeros(total_ref.shape, f32)
    for number, ref in enumerate((own_ref, other_ref)):
        part = slice(number * rows, (number + 1) * rows)
        grads = dot_right(ref[...], weight_ref[...]) * slope_ref[part, :].astype(f32)
        grads = grads.astype(bf16)
        result_ref[part, :] = grads
        total = total + jnp.sum(grads.astype(f32), axis=0, keepdims=True)
    total_ref[...] = total


def hidden_backward(weight, cot_own, cot_other, slopes):
    rows, width = cot_own.shape
    breadth = slopes.shape[1]
    tile = min(256, breadth)
    return pl.pallas_call(
        hidden_backward_kernel,
        grid=(breadth // tile,),
        in_specs=[
            whole_spec((rows, width)),
            whole_spec((rows, width)),
            pl.BlockSpec((tile, width), lambda step: (step, 0)),
            pl.BlockSpec((2 * rows, tile), lambda step: (0, step)),
        ],
        out_specs=[
            pl.BlockSpec((2 * rows, tile), lambda step: (0, step)),
            pl.BlockSpec((1, tile), lambda step: (0, step)),
        ],
        out_shape=[
            jax.ShapeDtypeStruct((2 * rows, breadth), bf16),
            jax.ShapeDtypeStruct((1, breadth), f32),
        ],
        compiler_params=pltpu.CompilerParams(
            dimension_semantics=("arbitrary",), vmem_limit_bytes=12 * 1024 * 1024
        ),
        cost_estimate=pl.CostEstimate(flops=1, bytes_accessed=1, transcendentals=0),
        name="hidden_backward",
    )(cot_own, cot_other, weight, slopes)


def up_backward_kernel(grads_ref, weight_ref, result_ref):
    result_ref[...] = dot_right(grads_ref[...], weight_ref[...]).astype(result_ref.dtype)


def up_backward(weight, grads, number, kind_of):
    rows, breadth = grads.shape[0] // 2, grads.shape[1]
    width = weight.shape[0]
    tile = width // 4
    return pl.pallas_call(
        up_backward_kernel,
        grid=(4,),
        in_specs=[
            pl.BlockSpec((rows, breadth), lambda step: (number, 0)),
            pl.BlockSpec((tile, breadth), lambda step: (step, 0)),
        ],
        out_specs=pl.BlockSpec((rows, tile), lambda step: (0, step)),
        out_shape=jax.ShapeDtypeStruct((rows, width), kind_of),
        compiler_params=pltpu.CompilerParams(
            dimension_semantics=("arbitrary",), vmem_limit_bytes=12 * 1024 * 1024
        ),
        cost_estimate=pl.CostEstimate(flops=1, bytes_accessed=1, transcendentals=0),
        name="up_backward",
    )(grads, weight)


def down_projection_kernel(hidden_ref, weight_ref, result_ref):
    result_ref[...] = dot(hidden_ref[...], weight_ref[...]).astype(result_ref.dtype)


def down_projection(hidden, weight):
    rows, breadth = hidden.shape
    width = weight.shape[1]
    tile = min(256, rows)
    return pl.pallas_call(
        down_projection_kernel,
        grid=(rows // tile,),
        in_specs=[
            pl.BlockSpec((tile, breadth), lambda step: (step, 0)),
            whole_spec((breadth, width)),
        ],
        out_specs=pl.BlockSpec((tile, width), lambda step: (step, 0)),
        out_shape=jax.ShapeDtypeStruct((rows, width), bf16),
        compiler_params=pltpu.CompilerParams(
            dimension_semantics=("arbitrary",), vmem_limit_bytes=14 * 1024 * 1024
        ),
        cost_estimate=pl.CostEstimate(flops=1, bytes_accessed=1, transcendentals=0),
        name="down_projection",
    )(hidden, weight)


def up_gradient_kernel(own_ref, other_ref, grads_ref, result_ref, act_turned):
    rows, width = own_ref.shape
    step = 256

    @pl.when(pl.program_id(0) == 0)
    def _():
        for number, ref in enumerate((own_ref, other_ref)):
            for row in range(0, rows, step):
                first = number * rows + row
                for column in range(0, width, step):
                    block = ref[row : row + step, column : column + step]
                    act_turned[column : column + step, first : first + step] = turned(block).astype(bf16)

    result_ref[...] = dot(act_turned[...], grads_ref[...]).astype(bf16)


def up_gradient(act_own, act_other, grads):
    rows, width = act_own.shape
    breadth = grads.shape[1]
    tile = min(512, breadth)
    return pl.pallas_call(
        up_gradient_kernel,
        grid=(breadth // tile,),
        in_specs=[
            whole_spec((rows, width)),
            whole_spec((rows, width)),
            pl.BlockSpec((2 * rows, tile), lambda step: (0, step)),
        ],
        out_specs=pl.BlockSpec((width, tile), lambda step: (0, step)),
        out_shape=jax.ShapeDtypeStruct((width, breadth), bf16),
        scratch_shapes=[pltpu.VMEM((width, 2 * rows), bf16)],
        compiler_params=pltpu.CompilerParams(
            dimension_semantics=("arbitrary",), vmem_limit_bytes=16 * 1024 * 1024
        ),
        cost_estimate=pl.CostEstimate(flops=1, bytes_accessed=1, transcendentals=0),
        name="up_gradient",
    )(act_own, act_other, grads)


def together(*values):
    return lax.optimization_barrier(tuple(values))


def ordered(own, other, bit, axis=0):
    first = jnp.where(bit == 0, own, other)
    second = jnp.where(bit == 0, other, own)
    return jnp.stack([first, second], axis=axis)


class Moves:
    def __init__(self):
        self.shards = lax.axis_size("shard")
        self.reps = lax.axis_size("rep")
        self.half = self.shards // 2
        self.chips = self.reps // 2
        self.shard = lax.axis_index("shard")
        self.rep = lax.axis_index("rep")
        self.core = self.rep & 1
        self.chip = self.rep >> 1
        self.side = lax.div(self.shard, self.half)
        self.member = lax.rem(self.shard, self.half) + self.core * self.half

    def core_swap(self, part):
        return lax.ppermute(part, "rep", [(r, r ^ 1) for r in range(self.reps)])

    def chip_swap(self, part, bits):
        return lax.ppermute(part, "rep", [(r, r ^ (2 * bits)) for r in range(self.reps)])

    def shard_swap(self, part, bits):
        return lax.ppermute(part, "shard", [(s, s ^ bits) for s in range(self.shards)])

    def shard_bit(self, bits):
        return lax.div(self.shard, bits) & 1

    def low_bits(self):
        bits, result = 1, []
        while bits < self.half:
            result.append(bits)
            bits *= 2
        return result

    def home_send(self, part):
        pairs = []
        for rep in range(self.reps):
            for shard in range(self.shards):
                if shard // self.half != rep % 2:
                    to_shard = (shard + self.half) % self.shards
                    pairs.append((rep * self.shards + shard, (rep ^ 1) * self.shards + to_shard))
        return lax.ppermute(part, ("rep", "shard"), pairs)

    def home_join(self, part, other):
        return jnp.where(self.side == self.core, part, other)

    def half_gather(self, part):
        stack = part[None]
        for bits in self.low_bits():
            own = stack
            stack = ordered(own, self.shard_swap(own, bits), self.shard_bit(bits))
            stack = stack.reshape((-1,) + part.shape)
        return stack

    def cores_gather(self, stack):
        stack = ordered(stack, self.core_swap(stack), self.core)
        return stack.reshape((-1,) + stack.shape[2:])

    def exchange_bit(self, stack, bit, swap):
        sources, targets = stack.shape[:2]
        stack = stack.reshape((sources, 2, targets // 2) + stack.shape[2:])
        own, other = pick(stack, bit, 1), swap(pick(stack, 1 - bit, 1))
        return ordered(own, other, bit, 1).reshape((2 * sources,) + own.shape[1:])

    def half_exchange(self, stack):
        stack = stack[None]
        for bits in reversed(self.low_bits()):
            swap = functools.partial(self.shard_swap, bits=bits)
            stack = self.exchange_bit(stack, self.shard_bit(bits), swap)
        return stack.reshape((self.half,) + stack.shape[2:])

    def cores_exchange(self, stack):
        return self.exchange_bit(stack[None], self.core, self.core_swap)

    def members_exchange(self, stack):
        for bits in reversed(self.low_bits()):
            swap = functools.partial(self.shard_swap, bits=bits)
            stack = self.exchange_bit(stack, self.shard_bit(bits), swap)
        return stack.reshape((self.shards,) + stack.shape[2:])

    def reduce_bit(self, stack, bit, swap):
        stack = stack.reshape((2, stack.shape[0] // 2) + stack.shape[1:])
        other = swap(pick(stack, 1 - bit).astype(bf16))
        return pick(stack, bit).astype(f32) + other.astype(f32)

    def spread_open(self, part):
        if self.chips == 4:
            return (self.chip_swap(part, 1), self.chip_swap(part, 2))
        held, bits = [part], 1
        while bits < self.chips:
            held = held + [self.chip_swap(piece, bits) for piece in held]
            bits *= 2
        return tuple(held[1:])

    def spread_close(self, state):
        if self.chips == 4:
            by_x, by_y = state
            cut, axis = by_x.shape[-2] // 2, by_x.ndim - 2
            far = [
                self.chip_swap(by_x[..., :cut, :], 2),
                self.chip_swap(by_y[..., cut:, :], 1),
            ]
            return (by_x, by_y, jnp.concatenate(far, axis=axis))
        return state

    def far_open(self, states):
        if self.chips != 4:
            return ()
        cut = states[0][0].shape[0] // 2
        return (
            self.chip_swap(jnp.concatenate([by_x[:cut] for by_x, _ in states], axis=0), 2),
            self.chip_swap(jnp.concatenate([by_y[cut:] for _, by_y in states], axis=0), 1),
        )

    def far_parts(self, states, far):
        if self.chips != 4:
            return [[(k + 1, 0, part) for k, part in enumerate(state)] for state in states]
        cut = states[0][0].shape[0] // 2
        result = []
        for number, (by_x, by_y) in enumerate(states):
            rows = slice(number * cut, (number + 1) * cut)
            result.append([(1, 0, by_x), (2, 0, by_y), (3, 0, far[0][rows]), (3, cut, far[1][rows])])
        return result

    def chips_gather(self, part, axis, state=None):
        shape = part.shape[:axis] + (self.chips,) + part.shape[axis:]
        stack = place(jnp.zeros(shape, part.dtype), part, self.chip, axis)
        others = self.spread_close(self.spread_open(part) if state is None else state)
        for number, piece in enumerate(others):
            stack = place(stack, piece, self.chip ^ (number + 1), axis)
        return stack

    def reduce_open(self, stack, axis):
        return self.reduce_start(self.reduce_cut(stack, axis), axis)

    def reduce_cut(self, stack, axis):
        if self.chips != 4:
            return (stack,)
        shape = stack.shape[:axis] + (2, 2) + stack.shape[axis + 1 :]
        stack = stack.reshape(shape)
        bit_x, bit_y = self.chip & 1, self.chip >> 1
        cut = shape[0] // 2
        first, second = stack[:cut], stack[cut:]
        return (
            pick(first, bit_x, axis + 1),
            pick(second, bit_y, axis),
            pick(first, 1 - bit_x, axis + 1),
            pick(second, 1 - bit_y, axis),
        )

    def reduce_start(self, parts, axis):
        if self.chips == 4:
            first, second, send_first, send_second = parts
            return (first, second, self.chip_swap(send_first, 1), self.chip_swap(send_second, 2))
        (stack,) = parts
        count = self.chips
        stack = stack.astype(f32)
        while count > 1:
            count //= 2
            shape = stack.shape[:axis] + (2, count) + stack.shape[axis + 1 :]
            stack = stack.reshape(shape)
            bit = lax.div(self.chip, count) & 1
            got = self.chip_swap(pick(stack, 1 - bit, axis).astype(bf16), count)
            stack = pick(stack, bit, axis) + got.astype(f32)
        return (pick(stack, 0, axis).astype(bf16),)

    def reduce_add(self, state):
        if self.chips != 4:
            return state
        first, second, got_first, got_second = state
        first = (first.astype(f32) + got_first.astype(f32)).astype(bf16)
        second = (second.astype(f32) + got_second.astype(f32)).astype(bf16)
        return (first, second)

    def reduce_send(self, state, axis):
        if self.chips != 4:
            return state
        first, second = state
        bit_x, bit_y = self.chip & 1, self.chip >> 1
        got_first = self.chip_swap(pick(first, 1 - bit_y, axis), 2)
        got_second = self.chip_swap(pick(second, 1 - bit_x, axis), 1)
        return (pick(first, bit_y, axis), pick(second, bit_x, axis), got_first, got_second)

    def reduce_final(self, state):
        if self.chips != 4:
            return state[0]
        first, second, got_first, got_second = state
        first = first.astype(f32) + got_first.astype(f32)
        second = second.astype(f32) + got_second.astype(f32)
        return jnp.concatenate([first, second], axis=0).astype(bf16)

    def reduce_close(self, state, axis):
        return self.reduce_final(self.reduce_send(state, axis))

    def core_pair(self, part):
        other = self.core_swap(part)
        first = jnp.where(self.core == 0, part, other)
        second = jnp.where(self.core == 0, other, part)
        return first, second

    def sum_reps(self, vector):
        bits = 1
        while bits < self.reps:
            vector = vector + lax.ppermute(vector, "rep", [(r, r ^ bits) for r in range(self.reps)])
            bits *= 2
        return vector

    def sum_shards(self, vector):
        bits = 1
        while bits < self.shards:
            vector = vector + self.shard_swap(vector, bits)
            bits *= 2
        return vector


def stats_kernel(decay_rate, gradient_ref, old_ref, rows_ref, lane_rows_ref, sums_ref, total_ref, partial):
    step = pl.program_id(0)
    rows, columns = gradient_ref.shape

    @pl.when(step == 0)
    def _():
        partial[...] = jnp.zeros_like(partial)
        total_ref[...] = jnp.zeros_like(total_ref)

    gradient = gradient_ref[...].astype(f32)
    square = gradient * gradient
    row_mean = jnp.sum(square, axis=1, keepdims=True) / columns
    old = jnp.transpose(jnp.broadcast_to(old_ref[...], (128, rows)))[:, 0:1]
    rows_new = decay_rate * old + (1.0 - decay_rate) * (row_mean + eps_second)
    rows_ref[...] = rows_new
    lane_rows_ref[...] = jnp.transpose(jnp.broadcast_to(rows_new, (rows, 128)))[0:1, :]
    total_ref[...] += jnp.broadcast_to(jnp.sum(rows_new, axis=0, keepdims=True), (1, 128))
    partial[0:8, :] += eights(square, jnp.sum)
    partial[8:16, :] += eights(square * (1.0 / rows_new), jnp.sum)

    @pl.when(step == pl.num_programs(0) - 1)
    def _():
        sums_ref[0:1, :] = jnp.sum(partial[0:8, :], axis=0, keepdims=True)
        sums_ref[1:2, :] = jnp.sum(partial[8:16, :], axis=0, keepdims=True)


def factor_stats(gradient, rows_old, decay_rate):
    height, breadth = gradient.shape
    rows = min(256 if breadth <= 1024 else 128, height)
    return pl.pallas_call(
        functools.partial(stats_kernel, decay_rate),
        grid=(height // rows,),
        in_specs=[
            pl.BlockSpec((rows, breadth), lambda step: (step, 0)),
            pl.BlockSpec((1, rows), lambda step: (0, step)),
        ],
        out_specs=[
            pl.BlockSpec((rows, 1), lambda step: (step, 0)),
            pl.BlockSpec((1, rows), lambda step: (0, step)),
            pl.BlockSpec((2, breadth), lambda step: (0, 0)),
            pl.BlockSpec((1, 128), lambda step: (0, 0)),
        ],
        out_shape=[
            jax.ShapeDtypeStruct((height, 1), f32),
            jax.ShapeDtypeStruct((1, height), f32),
            jax.ShapeDtypeStruct((2, breadth), f32),
            jax.ShapeDtypeStruct((1, 128), f32),
        ],
        scratch_shapes=[pltpu.VMEM((16, breadth), f32)],
        compiler_params=pltpu.CompilerParams(
            dimension_semantics=("arbitrary",), vmem_limit_bytes=12 * 1024 * 1024
        ),
        name="factor_stats",
    )(gradient, rows_old)


def apply_kernel(
    decay_rate,
    height,
    gradient_ref,
    weight_ref,
    rows_ref,
    sums_ref,
    scalar_ref,
    old_ref,
    gradient_out,
    weight_out,
    copy_out,
    cols_out,
    rms_out,
    col_factor,
):
    columns = gradient_ref.shape[1]

    @pl.when(pl.program_id(0) == 0)
    def _():
        cols_new = decay_rate * old_ref[...] + (1.0 - decay_rate) * (
            sums_ref[0:1, :] / height + eps_second
        )
        row_mean = scalar_ref[0:1, 0:1] / height
        weight_mean = scalar_ref[1:2, 0:1] / (height * columns)
        scaled = jnp.sum(sums_ref[1:2, :] / cols_new, axis=1, keepdims=True)
        rms_update = jnp.sqrt(row_mean / (height * columns) * scaled)
        factor = rate_step * jnp.sqrt(weight_mean) * jnp.sqrt(row_mean)
        factor = factor / jnp.maximum(1.0, rms_update / clip_level)
        col_factor[...] = factor * lax.rsqrt(cols_new)
        cols_out[...] = cols_new
        rms_out[...] = jnp.broadcast_to(rms_update, (1, 128))

    gradient = gradient_ref[...].astype(f32)
    new_weight = weight_ref[...] - gradient * lax.rsqrt(rows_ref[...]) * col_factor[...]
    gradient_out[...] = gradient
    weight_out[...] = new_weight
    copy_out[...] = new_weight.astype(bf16)


def factor_apply(gradient, weight, rows_new, sums, scalars, cols_old, height, decay_rate):
    own_height, breadth = gradient.shape
    rows = min(256 if breadth <= 1024 else 64, own_height)

    def rows_spec():
        return pl.BlockSpec((rows, breadth), lambda step: (step, 0))

    def row_spec(count, wide):
        return pl.BlockSpec((count, wide), lambda step: (0, 0))

    return pl.pallas_call(
        functools.partial(apply_kernel, decay_rate, height),
        grid=(own_height // rows,),
        in_specs=[
            rows_spec(),
            rows_spec(),
            pl.BlockSpec((rows, 1), lambda step: (step, 0)),
            row_spec(2, breadth),
            row_spec(2, 128),
            row_spec(1, breadth),
        ],
        out_specs=[rows_spec(), rows_spec(), rows_spec(), row_spec(1, breadth), row_spec(1, 128)],
        out_shape=[
            jax.ShapeDtypeStruct((own_height, breadth), f32),
            jax.ShapeDtypeStruct((own_height, breadth), f32),
            jax.ShapeDtypeStruct((own_height, breadth), bf16),
            jax.ShapeDtypeStruct((1, breadth), f32),
            jax.ShapeDtypeStruct((1, 128), f32),
        ],
        scratch_shapes=[pltpu.VMEM((1, breadth), f32)],
        compiler_params=pltpu.CompilerParams(
            dimension_semantics=("arbitrary",), vmem_limit_bytes=14 * 1024 * 1024
        ),
        name="factor_apply",
    )(gradient, weight, rows_new, sums, scalars, cols_old)


def summed(moves, entries):
    total = moves.sum_shards(jnp.concatenate(entries, axis=1))
    result, offset = [], 0
    for entry in entries:
        result.append(total[:, offset : offset + entry.shape[1]])
        offset += entry.shape[1]
    return result


def on_device(
    tokens,
    cotangent,
    seq_lengths,
    qkv_weight,
    out_weight,
    up_weight,
    down_weight,
    vectors,
    row_state,
    down_rows,
    col_state,
    vector_state,
):
    moves = Moves()
    shards, half, chips, core = moves.shards, moves.half, moves.chips, moves.core
    row_count, width = tokens.shape
    hidden_width = up_weight.shape[1]
    group_rows = row_count * shards
    heads = HEADS // shards
    head_width = width // HEADS
    span = heads * head_width
    member = moves.member
    decay_rate = 1.0 - STEP ** (-0.8)
    head_number = (member * heads + jnp.arange(heads, dtype=jnp.int32)).astype(f32)
    slopes = jnp.exp2(-8.0 * (head_number + 1.0) / HEADS)

    gain_one = vectors[0:width]
    shift_one = vectors[width : 2 * width]
    bias_query = vectors[2 * width : 3 * width]
    bias_value = vectors[3 * width : 4 * width]
    bias_out = vectors[4 * width : 5 * width]
    gain_two = vectors[5 * width : 6 * width]
    shift_two = vectors[6 * width : 7 * width]
    bias_up = vectors[7 * width : 7 * width + hidden_width]
    bias_down = vectors[7 * width + hidden_width :]

    other_tokens = moves.home_send(tokens)
    other_lengths = moves.core_swap(seq_lengths)
    lengths = jnp.where(moves.side == core, seq_lengths, other_lengths)[0]
    plan = block_plan(lengths, group_rows, BLOCK)
    rows_z = width // shards
    rows_piece = rows_z // chips
    my_rows = cut_rows(qkv_weight, moves.chip * rows_piece, rows_piece)
    my_rows = my_rows.astype(bf16)
    my_blocks = []
    for number in range(half):
        kinds = []
        for kind in range(3):
            first = kind * width + number * span
            second = first + half * span
            kinds.append(
                jnp.where(
                    core == 0, my_rows[:, first : first + span], my_rows[:, second : second + span]
                )
            )
        my_blocks.append(jnp.concatenate(kinds, axis=1))
    qkv_part = moves.half_exchange(jnp.stack(my_blocks))
    half_cols = hidden_width // (2 * shards)
    up_wide = shards * half_cols
    out_wide = width // 2
    down_piece = half_cols // chips

    def core_half(values):
        parts = []
        for number in range(shards):
            start = 2 * number * half_cols
            first = values[..., start : start + half_cols]
            second = values[..., start + half_cols : start + 2 * half_cols]
            parts.append(jnp.where(core == 0, first, second))
        return jnp.concatenate(parts, axis=-1)

    up_own = core_half(up_weight).astype(bf16).reshape(chips, rows_piece, up_wide)
    out_own = jnp.where(core == 0, out_weight[:, :out_wide], out_weight[:, out_wide:]).astype(bf16)
    out_own = out_own.reshape(chips, rows_piece, out_wide)
    down_own = cut_rows(down_weight, core * half_cols, half_cols).astype(bf16)
    fold = down_piece // rows_piece
    down_own = down_own.reshape(chips, fold, rows_piece, width)
    my_down = pick(down_own, moves.chip)
    weight_piece = jnp.concatenate(
        [pick(up_own, moves.chip), pick(out_own, moves.chip)] + [my_down[k] for k in range(fold)],
        axis=1,
    )
    near_pieces, bits = [weight_piece], 1
    while bits < half:
        near_pieces = near_pieces + [moves.shard_swap(piece, bits) for piece in near_pieces]
        bits *= 2
    near_pieces = near_pieces[1:]
    weights = [qkv_weight, out_weight, up_weight, down_weight]
    weight_sums = [jnp.sum(weight * weight) for weight in weights]
    other_tokens, qkv_part, near_pieces, weight_piece, plan, weight_sums = together(
        other_tokens, qkv_part, near_pieces, weight_piece, plan, weight_sums
    )
    home_tokens = moves.home_join(tokens, other_tokens)
    far_piece = moves.shard_swap(weight_piece, half)
    near_open = [moves.spread_open(piece) for piece in near_pieces]
    qkv_far = moves.shard_swap(qkv_part, half)
    qkv_far, near_open = together(qkv_far, near_open)
    qkv_part = ordered(qkv_part, qkv_far, moves.side).reshape(shards, rows_piece, 3 * span)
    qkv_cols = moves.chips_gather(qkv_part, 1).reshape(width, 3 * span)
    inputs = home_tokens.astype(f32)
    normed_one, inv_std_one = norm_parts(inputs)
    act_one = (normed_one * gain_one + shift_one).astype(bf16)
    act_half = moves.half_gather(act_one)

    act_half, qkv_cols, far_piece = together(act_half, qkv_cols, far_piece)
    near_far = moves.far_open(near_open)
    act_all = moves.cores_gather(act_half).reshape(group_rows, width)
    far_open = moves.spread_open(far_piece)
    far_pieces, bits = [far_piece], 1
    while bits < half:
        far_pieces = far_pieces + [moves.shard_swap(piece, bits) for piece in far_pieces]
        bits *= 2
    far_pieces = far_pieces[1:]

    bias_q_part = cut_rows(bias_query, member * span, span)
    bias_v_part = cut_rows(bias_value, member * span, span)
    qkv_bias = jnp.concatenate([bias_q_part, jnp.zeros_like(bias_q_part), bias_v_part])
    qkv_rows = (dot(act_all, qkv_cols) + qkv_bias).astype(bf16)
    attended_cols, logs = attend_forward(qkv_rows, plan, slopes, heads, BLOCK)
    attended_cols, far_open, far_pieces, near_far = together(
        attended_cols, far_open, far_pieces, near_far
    )
    attended_parts = moves.cores_exchange(attended_cols.reshape(shards, row_count, span))
    attended_parts = moves.members_exchange(attended_parts)
    second_far = moves.far_open([far_open])
    last_states = [moves.spread_open(piece) for piece in far_pieces]
    attended_parts, second_far, last_states, cotangent = together(
        attended_parts, second_far, last_states, cotangent
    )
    last_far = moves.far_open(last_states)
    other_cot = moves.home_send(cotangent)
    attended = jnp.concatenate([attended_parts[k] for k in range(shards)], axis=1)

    up_all = place(jnp.zeros((shards, chips, rows_piece, up_wide), bf16), up_own, moves.shard)
    out_all = place(jnp.zeros((shards, chips, rows_piece, out_wide), bf16), out_own, moves.shard)
    down_all = place(jnp.zeros((shards, chips, fold, rows_piece, width), bf16), down_own, moves.shard)
    pieces = near_pieces + [far_piece] + far_pieces
    parts_of = moves.far_parts(near_open, near_far) + moves.far_parts([far_open], second_far)
    parts_of += moves.far_parts(last_states, last_far)
    for number, (piece, parts) in enumerate(zip(pieces, parts_of)):
        plane = moves.shard ^ (number + 1)
        for far, row, rows in [(0, 0, piece)] + parts:
            chip = moves.chip ^ far
            up_all = lax.dynamic_update_slice(
                up_all, rows[None, None, :, :up_wide], (plane, chip, row, 0), allow_negative_indices=False
            )
            out_all = lax.dynamic_update_slice(
                out_all, rows[None, None, :, up_wide : up_wide + out_wide], (plane, chip, row, 0), allow_negative_indices=False
            )
            start = up_wide + out_wide
            folds = [rows[:, start + k * width : start + (k + 1) * width] for k in range(fold)]
            down_all = lax.dynamic_update_slice(
                down_all, jnp.stack(folds)[None, None], (plane, chip, 0, row, 0), allow_negative_indices=False
            )
    up_half = up_all.reshape(width, up_wide)
    down_half = down_all.reshape(up_wide, width)
    out_first, out_second = moves.core_pair(out_all.reshape(width, out_wide))
    out_low = jnp.concatenate([out_first, out_second], axis=1)
    residual = inputs + dot(attended, out_low) + bias_out
    normed_two, inv_std_two = norm_parts(residual)
    act_two = (normed_two * gain_two + shift_two).astype(bf16)

    act_two_other, attended_other = together(
        moves.core_swap(act_two), moves.core_swap(attended)
    )
    act_two_pair = jnp.concatenate([act_two, act_two_other], axis=0)
    attended_pair = jnp.concatenate([attended, attended_other], axis=0)
    bias_up_half = core_half(bias_up)
    up_pair = dot(act_two_pair, up_half) + bias_up_half
    hidden_pair = gelu_value(up_pair).astype(bf16)
    slope_pair = gelu_slope(up_pair).astype(bf16)
    hidden_pair, slope_pair, other_cot = together(hidden_pair, slope_pair, other_cot)
    home_cot = moves.home_join(cotangent, other_cot)
    cot_other = moves.core_swap(home_cot)
    cot_pair = jnp.concatenate([home_cot, cot_other], axis=0)
    down_terms = dot_rows(hidden_pair, cot_pair).astype(bf16)
    down_state = moves.reduce_cut(down_terms.reshape(shards, chips, down_piece, width), 1)
    slope_pair, down_state = together(slope_pair, down_state)
    down_state = moves.reduce_start(down_state, 1)
    grad_y = home_cot.astype(f32)
    grad_bias_down = jnp.sum(grad_y, axis=0)
    grad_up_pair, grad_bias_up = hidden_backward(down_half, home_cot, cot_other, slope_pair)
    grad_bias_up = grad_bias_up.reshape(-1)
    back_other = moves.core_swap(up_backward(up_half, grad_up_pair, 1, bf16))
    up_terms = up_gradient(act_two, act_two_other, grad_up_pair)
    down_pair = down_projection(hidden_pair, down_half)
    back_other, down_pair, up_terms, down_state = together(
        back_other, down_pair, up_terms, down_state
    )
    up_cut = moves.reduce_cut(up_terms.reshape(shards, chips, rows_piece, up_wide), 1)
    down_sums = moves.reduce_add(down_state)
    grad_act_two = up_backward(up_half, grad_up_pair, 0, f32) + back_other.astype(f32)
    grad_gain_two = jnp.sum(grad_act_two * normed_two, axis=0)
    grad_shift_two = jnp.sum(grad_act_two, axis=0)
    grad_residual = grad_y + norm_back(grad_act_two, normed_two, inv_std_two, gain_two)
    grad_attn = grad_residual.astype(bf16)
    grad_bias_out = jnp.sum(grad_attn, axis=0, dtype=f32)
    to_members = jnp.stack(
        [
            dot_right(grad_attn, out_low[k * span : (k + 1) * span]).astype(bf16)
            for k in range(shards)
        ]
    )
    attn_halves = [grad_attn[:, :out_wide], grad_attn[:, out_wide:]]
    attn_own = jnp.where(core == 0, attn_halves[0], attn_halves[1])
    attn_other = jnp.where(core == 0, attn_halves[1], attn_halves[0])
    down_other = moves.core_swap(down_pair[row_count:])
    grad_heads, attn_other, up_cut, down_sums, down_other = together(
        moves.cores_exchange(to_members), moves.core_swap(attn_other), up_cut, down_sums, down_other
    )
    attn_pair = jnp.concatenate([attn_own, attn_other], axis=0)
    grad_heads = moves.members_exchange(grad_heads).reshape(group_rows, span)
    up_state = moves.reduce_start(up_cut, 1)
    down_mid = moves.reduce_close(down_sums, 1)
    block_out = residual + down_pair[:row_count].astype(f32) + down_other.astype(f32) + bias_down
    block_out = block_out.astype(bf16)

    out_terms = dot_rows(attended_pair, attn_pair).astype(bf16)
    def shards_halve(piece, bits):
        piece = piece.reshape((piece.shape[0] // 2, 2) + piece.shape[1:])
        bit = moves.shard_bit(bits)
        return pick(piece, bit, 1), moves.shard_swap(pick(piece, 1 - bit, 1), bits)

    def halved(state):
        own, other = state
        return (own.astype(f32) + other.astype(f32)).astype(bf16)

    def shards_sum(piece):
        rows = piece.shape[1]
        return lax.psum_scatter(
            piece.reshape(shards * rows, piece.shape[2]), "shard", scatter_dimension=0, tiled=True
        )

    grad_heads, down_mid, out_terms, block_out = together(
        grad_heads, down_mid, out_terms, block_out
    )
    block_other = moves.home_send(block_out)
    down_owned = shards_sum(down_mid)
    out_state = moves.reduce_open(out_terms.reshape(shards, chips, rows_piece, out_wide), 1)
    attend_args = (plan, slopes)
    parts = 2 if heads % 4 == 0 else 1
    part_heads = heads // parts
    grad_qkv = attend_backward(
        qkv_rows, grad_heads, attended_cols, logs, *attend_args, part_heads, BLOCK, 0, None
    )
    grad_qkv, up_state, out_state = together(grad_qkv, up_state, out_state)
    up_sums, out_sums = moves.reduce_add(up_state), moves.reduce_add(out_state)
    grad_qkv, up_sums, out_sums = together(grad_qkv, up_sums, out_sums)
    up_out_state = [
        jnp.concatenate([up_part, out_part], axis=-1) for up_part, out_part in zip(up_sums, out_sums)
    ]
    if parts == 2:
        grad_qkv = attend_backward(
            qkv_rows, grad_heads, attended_cols, logs, *attend_args, part_heads, BLOCK, part_heads, grad_qkv
        )
    grad_qkv, up_out_state, block_other, down_owned = together(
        grad_qkv, moves.reduce_send(up_out_state, 1), block_other, down_owned
    )
    block_out = moves.home_join(block_out, block_other)
    up_out_piece = moves.reduce_final(up_out_state)
    up_out_state = shards_halve(up_out_piece, 1)

    grad_bias_q_part = jnp.sum(grad_qkv[:, :span], axis=0, dtype=f32)
    grad_bias_v_part = jnp.sum(grad_qkv[:, 2 * span :], axis=0, dtype=f32)

    grad_halves = grad_qkv.reshape(2, half * row_count, 3 * span)
    sent = dot_right(pick(grad_halves, 1 - core), qkv_cols).astype(bf16)
    sent = moves.core_swap(sent)
    qkv_terms = dot_rows(act_all, grad_qkv).astype(bf16)
    qkv_terms = qkv_terms.reshape(shards, chips, rows_piece, 3 * span)
    qkv_state = moves.reduce_open(qkv_terms, 1)
    back = dot_right(pick(grad_halves, core), qkv_cols) + sent.astype(f32)
    qkv_state, back = together(qkv_state, back)

    back = back.reshape(half, row_count, width)
    low_bits = list(reversed(moves.low_bits()))
    for bits in low_bits[:-1]:
        back = moves.reduce_bit(
            back, moves.shard_bit(bits), functools.partial(moves.shard_swap, bits=bits)
        )
    back = back.reshape((2, -1) + back.shape[1:])
    back_bit = moves.shard_bit(low_bits[-1])
    back_other = moves.shard_swap(pick(back, 1 - back_bit).astype(bf16), low_bits[-1])
    qkv_state = moves.reduce_send(moves.reduce_add(qkv_state), 1)
    qkv_state, up_out_state = together(qkv_state, up_out_state)

    up_out_piece, bits = halved(up_out_state), 2
    while bits < half:
        up_out_piece = halved(shards_halve(up_out_piece, bits))
        bits *= 2
    up_out_state = shards_halve(up_out_piece, half)
    qkv_piece = moves.reduce_final(qkv_state)
    qkv_piece = qkv_piece.reshape((2, half) + qkv_piece.shape[1:])
    qkv_own = pick(qkv_piece, moves.side)
    qkv_other = moves.shard_swap(pick(qkv_piece, 1 - moves.side), half)
    back_other, qkv_other, up_out_state, down_owned = together(
        back_other, qkv_other, up_out_state, down_owned
    )

    up_out_owned = halved(up_out_state)[0]
    up_out_state = moves.spread_open(up_out_owned)
    qkv_piece = moves.half_exchange(halved((qkv_own, qkv_other)))
    down_state = moves.spread_open(down_owned)
    grad_act_one = pick(back, back_bit) + back_other.astype(f32)
    grad_act_one = grad_act_one.reshape(row_count, width)
    grad_gain_one = jnp.sum(grad_act_one * normed_one, axis=0)
    grad_shift_one = jnp.sum(grad_act_one, axis=0)
    grad_inputs = grad_residual + norm_back(grad_act_one, normed_one, inv_std_one, gain_one)
    grad_inputs, grad_gain_one, grad_shift_one, qkv_piece, down_state, up_out_state = together(
        grad_inputs.astype(bf16), grad_gain_one, grad_shift_one, qkv_piece, down_state, up_out_state
    )
    tokens_other = moves.home_send(grad_inputs)
    qkv_owned = moves.chips_gather(qkv_piece, 1)

    up_out_first, up_out_second = moves.core_pair(
        moves.chips_gather(up_out_owned, 0, tuple(up_out_state)).reshape(rows_z, up_wide + out_wide)
    )
    out_grad = jnp.concatenate([up_out_first[:, up_wide:], up_out_second[:, up_wide:]], axis=1)
    up_columns = []
    for number in range(shards):
        part = slice(number * half_cols, (number + 1) * half_cols)
        up_columns += [up_out_first[:, part], up_out_second[:, part]]
    up_grad = jnp.concatenate(up_columns, axis=1)
    down_first, down_second = moves.core_pair(
        moves.chips_gather(down_owned, 0, tuple(down_state)).reshape(half_cols, width)
    )
    down_grad = jnp.concatenate([down_first, down_second], axis=0)
    qkv_owned = qkv_owned.reshape(half, rows_z, 3 * span)
    qkv_other, tokens_other = together(moves.core_swap(qkv_owned), tokens_other)
    tokens_grad = moves.home_join(grad_inputs, tokens_other)
    qkv_first = jnp.where(core == 0, qkv_owned, qkv_other)
    qkv_second = jnp.where(core == 0, qkv_other, qkv_owned)
    qkv_columns = []
    for kind in range(3):
        for source in (qkv_first, qkv_second):
            for number in range(half):
                qkv_columns.append(source[number][:, kind * span : (kind + 1) * span])
    qkv_grad = jnp.concatenate(qkv_columns, axis=1)

    gradients = [qkv_grad, out_grad, up_grad, down_grad]
    heights = [width, width, width, hidden_width]
    rows_old = [row_state[k : k + 1] for k in range(3)] + [down_rows.reshape(1, -1)]
    stats = [
        factor_stats(gradient, old, decay_rate) for gradient, old in zip(gradients, rows_old)
    ]

    def to_sum(number):
        weight_sum = jnp.broadcast_to(weight_sums[number], (1, 128))
        return [stats[number][2], jnp.concatenate([stats[number][3], weight_sum], axis=0)]

    def spread_heads(part):
        return [jnp.where(member == number, part, 0.0) for number in range(shards)]

    bias_up_parts = []
    for number in range(shards):
        part = grad_bias_up[number * half_cols : (number + 1) * half_cols]
        bias_up_parts += [jnp.where(core == 0, part, 0.0), jnp.where(core == 1, part, 0.0)]
    vector_part = moves.sum_reps(
        jnp.concatenate(
            [grad_gain_one, grad_shift_one]
            + spread_heads(grad_bias_q_part)
            + spread_heads(grad_bias_v_part)
            + [grad_bias_out, grad_gain_two, grad_shift_two]
            + bias_up_parts
            + [grad_bias_down]
        )
    )
    vector_rows = vector_part.reshape(2, -1)
    all_sums = summed(moves, to_sum(0) + to_sum(1) + to_sum(2) + to_sum(3) + [vector_rows])
    sums = [all_sums[0:2], all_sums[2:4], all_sums[4:6], all_sums[6:8]]
    vector_grad = all_sums[8].reshape(-1)
    updates = []
    offset = 0
    for number in range(4):
        end_col = offset + gradients[number].shape[1]
        updates.append(
            factor_apply(
                gradients[number],
                weights[number],
                stats[number][0],
                sums[number][0],
                sums[number][1],
                col_state[offset:end_col].reshape(1, -1),
                heights[number],
                decay_rate,
            )
        )
        offset = end_col
    grads_out, new_weights, copies, new_cols, rms_rows = zip(*updates)
    rms_values = [rms[0, 0] for rms in rms_rows]

    vector_state_new = decay_rate * vector_state + (1.0 - decay_rate) * (
        vector_grad * vector_grad + eps_second
    )
    vector_step = vector_grad * lax.rsqrt(vector_state_new)
    vector_rms = jnp.sqrt(jnp.mean(vector_step * vector_step))
    vector_new = vectors - rate_step * jnp.sqrt(
        jnp.mean(vectors * vectors)
    ) * vector_step / jnp.maximum(1.0, vector_rms / clip_level)
    update_rms = jnp.stack(rms_values + [vector_rms])
    return (
        block_out,
        tokens_grad,
        *grads_out,
        vector_grad,
        *new_weights,
        vector_new,
        *copies,
        jnp.concatenate([stats[0][1], stats[1][1], stats[2][1]], axis=0),
        stats[3][1].reshape(-1),
        jnp.concatenate(new_cols, axis=1).reshape(-1),
        vector_state_new,
        update_rms,
    )


def solution(mesh):
    in_specs = (
        P(("rep", "shard"), None),
        P(("rep", "shard"), None),
        P("rep", None),
        P("shard", None),
        P("shard", None),
        P("shard", None),
        P("shard", None),
        P(),
        P(None, "shard"),
        P("shard"),
        P(),
        P(),
    )
    out_specs = (
        P(("rep", "shard"), None),
        P(("rep", "shard"), None),
        P("shard", None),
        P("shard", None),
        P("shard", None),
        P("shard", None),
        P(),
        P("shard", None),
        P("shard", None),
        P("shard", None),
        P("shard", None),
        P(),
        P("shard", None),
        P("shard", None),
        P("shard", None),
        P("shard", None),
        P(None, "shard"),
        P("shard"),
        P(),
        P(),
        P(),
    )
    return jax.shard_map(
        on_device, mesh=mesh, in_specs=in_specs, out_specs=out_specs, check_vma=False
    )
```

profile of v0, /device:TPU:0, one launch (start us, length us, event | category | flops | bytes accessed | tf_op | source)
XLA Modules:
  0.0 497.8 jit_solution(11273908048977565742)
XLA Ops:
  10.3 2.7 collective-permute-start.1
  14.7 2.4 select_convert_fusion.1
  19.8 4.0 multiply_reduce_fusion
  30.9 2.0 copy-done.6
  34.6 11.0 %collective-permute-done.2 = bf16[64,4608]{1,0:T(8,128)(2,1)} collective-permute-done((bf16[64,4608]{1,0:T(8,128)(2,1)}, bf16[64,4608]{1,0:T(8,128)(2,1)}, u32[]{:S(2)}, u32[]{:S(2)}) %collective-permute-start.2) | collective-permute-done | bytes 589856 | tf_op jit(solution)/shard_map/ppermute | solution.py:569
  49.1 2.5 collective-permute-start.12
  56.6 17.0 %collective-permute-done.5 = bf16[2,64,768]{2,1,0:T(8,128)(2,1)S(1)} collective-permute-done((bf16[2,64,768]{2,1,0:T(8,128)(2,1)S(1)}, bf16[2,64,768]{2,1,0:T(8,128)(2,1)S(1)}, u32[]{:S(2)}, u32[]{:S(2)}) %collective-permute-start.5) | collective-permute-done | bytes 196640 | tf_op jit(solution)/shard_map/ppermute | solution.py:569
  75.9 9.0 %collective-permute-done.9 = bf16[4,64,768]{2,1,0:T(8,128)(2,1)S(1)} collective-permute-done((bf16[4,64,768]{2,1,0:T(8,128)(2,1)S(1)}, bf16[4,64,768]{2,1,0:T(8,128)(2,1)S(1)}, u32[]{:S(2)}, u32[]{:S(2)}) %collective-permute-start.9) | collective-permute-done | bytes 393248 | tf_op jit(solution)/shard_map/ppermute | solution.py:566
  86.8 9.9 %collective-permute-done.4 = bf16[1,512,1024]{2,1,0:T(8,128)(2,1)S(1)} collective-permute-done((bf16[1,512,1024]{2,1,0:T(8,128)(2,1)S(1)}, bf16[1,512,1024]{2,1,0:T(8,128)(2,1)S(1)}, u32[]{:S(2)}, u32[]{:S(2)}) %collective-permute-start.4) | collective-permute-done | bytes 1048608 | tf_op jit(solution)/shard_map/ppermute | solution.py:569
  103.4 3.9 add_convert_fusion.1.qkv_ref.refs_5_
  107.3 22.4 %attend_forward.1 = (bf16[2048,256]{1,0:T(8,128)(2,1)S(1)}, f32[8,4,256]{2,1,0:T(4,128)S(1)}) custom-call(s32[8]{0:T(128)S(1)} %get-tuple-element.169.low_ref, s32[8]{0:T(128)S(1)} %get-tuple-element.170.mid_ref, f32[4]{0:T(128)S(1)} %multiply_exponential_fusion.slope_ref.refs_2_, s32[8,1,256]{2,1,0:T(1,128)S(1)} %bitcast.585, ...), custom_call_target="tpu_custom_call" | custom-call | flops 12884901888 | bytes 5242880 | tf_op jit(solution)/shard_map/attend_forward/pallas_call | solution.py:331
  136.3 2.0 collective-permute-start.20
  138.4 12.1 %collective-permute-done.20 = bf16[2,1,512,256]{3,2,0,1:T(8,128)(2,1)S(1)} collective-permute-done((bf16[2,1,512,256]{3,2,0,1:T(8,128)(2,1)S(1)}, bf16[2,1,512,256]{3,2,0,1:T(8,128)(2,1)S(1)}, u32[]{:S(2)}, u32[]{:S(2)}) %collective-permute-start.20) | collective-permute-done | bytes 524320 | tf_op jit(solution)/shard_map/ppermute | solution.py:569
  156.0 4.7 collective-permute-done.25
  161.0 2.5 collective-permute-done.27
  166.8 2.4 collective-permute-done.28.other_ref
  169.2 13.1 %add_convert_fusion = (bf16[1024,2048]{1,0:T(8,128)(2,1)S(1)}, bf16[1024,2048]{1,0:T(8,128)(2,1)S(1)}) fusion(f32[2048]{0:T(1024)S(1)} %pad_maximum_fusion.17, bf16[1024,2048]{1,0:T(8,128)(2,1)S(1)} %bitcast.570, bf16[512,1024]{1,0:T(8,128)(2,1)S(1)} %collective-permute-done.28.other_ref, bf16[512,1024]{1,0:T(8,128)(2,1)S(1)} %add_convert_fusion.7.own_ref), kind=kOutput, calls=%fused_computation.9 | convolution fusion | flops 4353687552 | bytes 14688256 | tf_op jit(solution)/shard_map/dot_general | solution.py:54
  184.2 2.1 collective-permute-done.31.other_ref
  186.3 4.9 convolution_convert_fusion
  194.4 7.5 %hidden_backward.1 = (bf16[1024,2048]{1,0:T(8,128)(2,1)S(1)}, f32[1,2048]{1,0:T(1,128)S(1)}) custom-call(bf16[512,1024]{1,0:T(8,128)(2,1)S(1)} %get-tuple-element.331.own_ref, bf16[512,1024]{1,0:T(8,128)(2,1)S(1)} %collective-permute-done.31.other_ref, bf16[2048,1024]{1,0:T(8,128)(2,1)S(1)} %bitcast.573, bf16[1024,2048]{1,0:T(8,128)(2,1)S(1)} %get-tuple-element.199.slope_ref), custom_call_target="tpu_custom_call" | custom-call | flops 1 | bytes 1 | tf_op jit(solution)/shard_map/hidden_backward/pallas_call | solution.py:425
  201.9 4.2 up_backward.3
  210.0 2.2 copy-done.9
  212.2 2.2 copy-done.24
  214.4 5.0 %down_projection.1 = bf16[1024,1024]{1,0:T(8,128)(2,1)S(1)} custom-call(bf16[1024,2048]{1,0:T(8,128)(2,1)S(1)} %copy-done.24, bf16[2048,1024]{1,0:T(8,128)(2,1)S(1)} %bitcast.574), custom_call_target="tpu_custom_call" | custom-call | flops 1 | bytes 1 | tf_op jit(solution)/shard_map/down_projection/pallas_call | solution.py:483
  219.5 3.1 up_backward.2
  222.6 6.4 %up_gradient.1 = bf16[1024,2048]{1,0:T(8,128)(2,1)S(1)} custom-call(bf16[512,1024]{1,0:T(8,128)(2,1)S(1)} %add_convert_fusion.7.own_ref, bf16[512,1024]{1,0:T(8,128)(2,1)S(1)} %collective-permute-done.28.other_ref, bf16[1024,2048]{1,0:T(8,128)(2,1)S(1)} %copy-done.1), custom_call_target="tpu_custom_call" | custom-call | flops 1 | bytes 1 | tf_op jit(solution)/shard_map/up_gradient/pallas_call | solution.py:520
  229.0 3.9 collective-permute-done.34
  233.7 2.3 multiply_reduce_fusion.3
  236.0 3.7 convert_reduce_fusion.2
  257.0 8.8 %collective-permute-done.38 = bf16[2,1,512,256]{3,2,0,1:T(8,128)(2,1)S(1)} collective-permute-done((bf16[2,1,512,256]{3,2,0,1:T(8,128)(2,1)S(1)}, bf16[2,1,512,256]{3,2,0,1:T(8,128)(2,1)S(1)}, u32[]{:S(2)}, u32[]{:S(2)}) %collective-permute-start.38) | collective-permute-done | bytes 524320 | tf_op jit(solution)/shard_map/ppermute | solution.py:569
  275.0 20.4 %attend_backward.2.refs_8_ = bf16[2048,384]{1,0:T(8,128)(2,1)S(1)} custom-call(s32[8]{0:T(128)S(1)} %get-tuple-element.219.refs_0_, s32[8]{0:T(128)S(1)} %get-tuple-element.220.refs_1_, f32[4]{0:T(128)S(1)} %multiply_exponential_fusion.slope_ref.refs_2_, s32[8,1,256]{2,1,0:T(1,128)S(1)} %bitcast.586, f32[8,4,256]{2,1,0:T(4,128)S(1)} %get-tuple-element.221.refs_4_, ...), custom_call_target="tpu_custom_call" | custom-call | flops 17179869184 | bytes 5242880 | tf_op jit(solution)/shard_map/attend_backward/pallas_call | solution.py:380
  303.2 20.8 %attend_backward.3 = bf16[2048,768]{1,0:T(8,128)(2,1)S(1)} custom-call(s32[8]{0:T(128)S(1)} %get-tuple-element.219.refs_0_, s32[8]{0:T(128)S(1)} %get-tuple-element.220.refs_1_, f32[4]{0:T(128)S(1)} %multiply_exponential_fusion.slope_ref.refs_2_, s32[8,1,256]{2,1,0:T(1,128)S(1)} %bitcast.587, f32[8,4,256]{2,1,0:T(4,128)S(1)} %get-tuple-element.221.refs_4_, ...), custom_call_target="tpu_custom_call" | custom-call | flops 17179869184 | bytes 5242880 | tf_op jit(solution)/shard_map/attend_backward/pallas_call | solution.py:380
  324.1 5.7 %convolution_convert_fusion.2 = bf16[1024,768]{1,0:T(8,128)(2,1)S(1)} fusion(bf16[2048,1024]{1,0:T(8,128)(2,1)} %bitcast.603, bf16[2048,768]{1,0:T(8,128)(2,1)S(1)} %attend_backward.3), kind=kOutput, calls=%fused_computation.90 | convolution fusion | flops 3222011904 | bytes 8912896 | tf_op jit(solution)/shard_map/dot_general | solution.py:64
  345.9 8.5 %collective-permute-done.54 = bf16[2,64,2560]{2,1,0:T(8,128)(2,1)S(1)} collective-permute-done((bf16[2,64,2560]{2,1,0:T(8,128)(2,1)S(1)}, bf16[2,64,2560]{2,1,0:T(8,128)(2,1)S(1)}, u32[]{:S(2)}, u32[]{:S(2)}) %collective-permute-start.54) | collective-permute-done | bytes 655392 | tf_op jit(solution)/shard_map/ppermute | solution.py:569
  355.4 2.5 collective-permute-start.55
  358.2 27.3 %collective-permute-done.55 = bf16[2,64,768]{2,1,0:T(8,128)(2,1)S(1)} collective-permute-done((bf16[2,64,768]{2,1,0:T(8,128)(2,1)S(1)}, bf16[2,64,768]{2,1,0:T(8,128)(2,1)S(1)}, u32[]{:S(2)}, u32[]{:S(2)}) %collective-permute-start.55) | collective-permute-done | bytes 196640 | tf_op jit(solution)/shard_map/ppermute | solution.py:569
  385.4 2.2 collective-permute-done.51
  397.7 3.1 collective-permute-done.57
  413.6 3.3 collective-permute-done.65
  422.6 3.2 collective-permute-done.71
  427.0 3.0 collective-permute-done.76
  438.3 2.4 factor_stats.7
  451.0 3.4 collective-permute-done.77
  454.5 3.1 collective-permute-start.78
  459.3 4.2 collective-permute-done.78
  473.6 4.2 factor_apply.4
  478.7 5.5 %factor_apply.7 = (f32[1024,1024]{1,0:T(8,128)}, f32[1024,1024]{1,0:T(8,128)}, bf16[1024,1024]{1,0:T(8,128)(2,1)}, f32[1,1024]{1,0:T(1,128)S(1)}, f32[1,128]{1,0:T(1,128)S(1)}) custom-call(bf16[1024,1024]{1,0:T(8,128)(2,1)S(1)} %pad_maximum_fusion.3.gradient_ref, f32[1024,1024]{1,0:T(8,128)S(1)} %copy-done.12, f32[1024,1]{1,0:T(8,128)S(1)} %copy-done.31, ...), custom_call_target="tpu_custom_call" | custom-call | tf_op jit(solution)/shard_map/factor_apply/pallas_call | solution.py:868
  484.9 4.2 factor_apply.6
  (629 shorter events, 171.9 us)
Async XLA Ops:
  7.2 316.9 %reduce-scatter.2.cloned.1.call-start = ((), (), s32[]{:S(2)}) async-start(), calls=%async_computation.1 | async-start | bytes 1310720 | tf_op jit(solution)/shard_map/reduce_scatter | solution.py:1134
  7.2 25.7 %collective-permute-start.3 = (s32[1,4]{1,0:T(1,128)}, s32[1,4]{1,0:T(1,128)S(1)}, u32[]{:S(2)}, u32[]{:S(2)}) collective-permute-start(s32[1,4]{1,0:T(1,128)} %param.14), channel_id=1, source_target_pairs={{0,4},{4,0},{8,12},{12,8},{16,20},{20,16},{24,28},{28,24},{1,5},{5... | collective-permute-start | bytes 56 | tf_op jit(solution)/shard_map/ppermute | solution.py:563
  10.3 23.3 %collective-permute-start.1 = (bf16[1,1,64,768]{3,2,1,0:T(8,128)(2,1)}, bf16[1,1,64,768]{3,2,1,0:T(8,128)(2,1)}, u32[]{:S(2)}, u32[]{:S(2)}) collective-permute-start(bf16[1,1,64,768]{3,2,1,0:T(8,128)(2,1)} %fusion.105), channel_id=1, source_target_pairs={{0,1},{1,0},{2,3},{3,2},{4,5},{5,4},{6,7},{7,6},{8,9},{9,8},{10,11... | collective-permute-start | bytes 294920 | tf_op jit(solution)/shard_map/ppermute | solution.py:569
  13.0 32.6 %collective-permute-start = (bf16[512,1024]{1,0:T(8,128)(2,1)}, bf16[512,1024]{1,0:T(8,128)(2,1)}, u32[]{:S(2)}, u32[]{:S(2)}) collective-permute-start(bf16[512,1024]{1,0:T(8,128)(2,1)} %param.12), channel_id=1, source_target_pairs={{2,4},{3,5},{4,2},{5,3},{10,12},{11,13},{12,10},{13,11},{18,20},{1... | collective-permute-start | bytes 3145736 | tf_op jit(solution)/shard_map/ppermute | solution.py:588
  19.8 25.9 %collective-permute-start.2 = (bf16[64,4608]{1,0:T(8,128)(2,1)}, bf16[64,4608]{1,0:T(8,128)(2,1)}, u32[]{:S(2)}, u32[]{:S(2)}) collective-permute-start(bf16[64,4608]{1,0:T(8,128)(2,1)} %pad_maximum_fusion.12), channel_id=1, source_target_pairs={{0,1},{1,0},{2,3},{3,2},{4,5},{5,4},{6,7},{7,6},{8,9},{9,8},{10,11... | collective-permute-start | bytes 1769480 | tf_op jit(solution)/shard_map/ppermute | solution.py:569
  45.7 28.0 %collective-permute-start.7 = (bf16[64,4608]{1,0:T(8,128)(2,1)}, bf16[64,4608]{1,0:T(8,128)(2,1)S(1)}, u32[]{:S(2)}, u32[]{:S(2)}) collective-permute-start(bf16[64,4608]{1,0:T(8,128)(2,1)} %collective-permute-done.2), channel_id=1, source_target_pairs={{0,16},{4,20},{8,24},{12,28},{16,0},{20,4},{24,8},{28,12},{1,17},{... | collective-permute-start | bytes 1769480 | tf_op jit(solution)/shard_map/ppermute | solution.py:566
  47.2 26.4 %collective-permute-start.6 = (bf16[64,4608]{1,0:T(8,128)(2,1)}, bf16[64,4608]{1,0:T(8,128)(2,1)S(1)}, u32[]{:S(2)}, u32[]{:S(2)}) collective-permute-start(bf16[64,4608]{1,0:T(8,128)(2,1)} %collective-permute-done.2), channel_id=1, source_target_pairs={{0,8},{4,12},{8,0},{12,4},{16,24},{20,28},{24,16},{28,20},{1,9},{5... | collective-permute-start | bytes 1769480 | tf_op jit(solution)/shard_map/ppermute | solution.py:566
  48.7 24.9 %collective-permute-start.5 = (bf16[2,64,768]{2,1,0:T(8,128)(2,1)S(1)}, bf16[2,64,768]{2,1,0:T(8,128)(2,1)S(1)}, u32[]{:S(2)}, u32[]{:S(2)}) collective-permute-start(bf16[2,64,768]{2,1,0:T(8,128)(2,1)S(1)} %maximum_bitcast_fusion.14), channel_id=1, source_target_pairs={{0,2},{1,3},{2,0},{3,1},{4,6},{5,7},{6,4},{7,5},{8,10},{9,11},{10,... | collective-permute-start | bytes 589832 | tf_op jit(solution)/shard_map/ppermute | solution.py:569
  49.1 48.6 %collective-permute-start.12 = (bf16[64,4608]{1,0:T(8,128)(2,1)}, bf16[64,4608]{1,0:T(8,128)(2,1)S(1)}, u32[]{:S(2)}, u32[]{:S(2)}) collective-permute-start(bf16[64,4608]{1,0:T(8,128)(2,1)} %pad_maximum_fusion.12), channel_id=1, source_target_pairs={{0,2},{1,3},{2,0},{3,1},{4,6},{5,7},{6,4},{7,5},{8,10},{9,11},{10,... | collective-permute-start | bytes 1769480 | tf_op jit(solution)/shard_map/ppermute | solution.py:569
  54.3 42.3 %collective-permute-start.4 = (bf16[1,512,1024]{2,1,0:T(8,128)(2,1)S(1)}, bf16[1,512,1024]{2,1,0:T(8,128)(2,1)S(1)}, u32[]{:S(2)}, u32[]{:S(2)}) collective-permute-start(bf16[1,512,1024]{2,1,0:T(8,128)(2,1)S(1)} %fusion.54), channel_id=1, source_target_pairs={{0,1},{1,0},{2,3},{3,2},{4,5},{5,4},{6,7},{7,6},{8,9},{9,8},{10,11... | collective-permute-start | bytes 3145736 | tf_op jit(solution)/shard_map/ppermute | solution.py:569
  84.9 12.7 %collective-permute-start.11 = (bf16[4,32,768]{2,1,0:T(8,128)(2,1)S(1)}, bf16[4,32,768]{2,1,0:T(8,128)(2,1)S(1)}, u32[]{:S(2)}, u32[]{:S(2)}) collective-permute-start(bf16[4,32,768]{2,1,0:T(8,128)(2,1)S(1)} %slice.828), channel_id=1, source_target_pairs={{0,8},{4,12},{8,0},{12,4},{16,24},{20,28},{24,16},{28,20},{1,9},{5... | collective-permute-start | bytes 589832 | tf_op jit(solution)/shard_map/ppermute | solution.py:566
  85.5 12.1 %collective-permute-start.10 = (bf16[4,32,768]{2,1,0:T(8,128)(2,1)S(1)}, bf16[4,32,768]{2,1,0:T(8,128)(2,1)S(1)}, u32[]{:S(2)}, u32[]{:S(2)}) collective-permute-start(bf16[4,32,768]{2,1,0:T(8,128)(2,1)S(1)} %slice.827), channel_id=1, source_target_pairs={{0,16},{4,20},{8,24},{12,28},{16,0},{20,4},{24,8},{28,12},{1,17},{... | collective-permute-start | bytes 589832 | tf_op jit(solution)/shard_map/ppermute | solution.py:566
  97.9 31.8 %collective-permute-start.18 = (bf16[32,4608]{1,0:T(8,128)(2,1)S(1)}, bf16[32,4608]{1,0:T(8,128)(2,1)S(1)}, u32[]{:S(2)}, u32[]{:S(2)}) collective-permute-start(bf16[32,4608]{1,0:T(8,128)(2,1)S(1)} %slice.652), channel_id=1, source_target_pairs={{0,8},{4,12},{8,0},{12,4},{16,24},{20,28},{24,16},{28,20},{1,9},{5... | collective-permute-start | bytes 884744 | tf_op jit(solution)/shard_map/ppermute | solution.py:566
  98.5 31.2 %collective-permute-start.17 = (bf16[32,4608]{1,0:T(8,128)(2,1)S(1)}, bf16[32,4608]{1,0:T(8,128)(2,1)S(1)}, u32[]{:S(2)}, u32[]{:S(2)}) collective-permute-start(bf16[32,4608]{1,0:T(8,128)(2,1)S(1)} %slice.651), channel_id=1, source_target_pairs={{0,16},{4,20},{8,24},{12,28},{16,0},{20,4},{24,8},{28,12},{1,17},{... | collective-permute-start | bytes 884744 | tf_op jit(solution)/shard_map/ppermute | solution.py:566
  99.2 30.6 %collective-permute-start.16 = (bf16[64,4608]{1,0:T(8,128)(2,1)S(1)}, bf16[64,4608]{1,0:T(8,128)(2,1)S(1)}, u32[]{:S(2)}, u32[]{:S(2)}) collective-permute-start(bf16[64,4608]{1,0:T(8,128)(2,1)S(1)} %collective-permute-done.12), channel_id=1, source_target_pairs={{0,1},{1,0},{2,3},{3,2},{4,5},{5,4},{6,7},{7,6},{8,9},{9,8},{10,11... | collective-permute-start | bytes 1769480 | tf_op jit(solution)/shard_map/ppermute | solution.py:569
  99.2 30.5 %collective-permute-start.15 = (bf16[64,4608]{1,0:T(8,128)(2,1)S(1)}, bf16[64,4608]{1,0:T(8,128)(2,1)S(1)}, u32[]{:S(2)}, u32[]{:S(2)}) collective-permute-start(bf16[64,4608]{1,0:T(8,128)(2,1)S(1)} %collective-permute-done.12), channel_id=1, source_target_pairs={{0,16},{4,20},{8,24},{12,28},{16,0},{20,4},{24,8},{28,12},{1,17},{... | collective-permute-start | bytes 1769480 | tf_op jit(solution)/shard_map/ppermute | solution.py:566
  101.9 27.8 %collective-permute-start.14 = (bf16[64,4608]{1,0:T(8,128)(2,1)S(1)}, bf16[64,4608]{1,0:T(8,128)(2,1)S(1)}, u32[]{:S(2)}, u32[]{:S(2)}) collective-permute-start(bf16[64,4608]{1,0:T(8,128)(2,1)S(1)} %collective-permute-done.12), channel_id=1, source_target_pairs={{0,8},{4,12},{8,0},{12,4},{16,24},{20,28},{24,16},{28,20},{1,9},{5... | collective-permute-start | bytes 1769480 | tf_op jit(solution)/shard_map/ppermute | solution.py:566
  129.9 21.7 %collective-permute-start.24 = (bf16[64,4608]{1,0:T(8,128)(2,1)S(1)}, bf16[64,4608]{1,0:T(8,128)(2,1)S(1)}, u32[]{:S(2)}, u32[]{:S(2)}) collective-permute-start(bf16[64,4608]{1,0:T(8,128)(2,1)S(1)} %collective-permute-done.16), channel_id=1, source_target_pairs={{0,16},{4,20},{8,24},{12,28},{16,0},{20,4},{24,8},{28,12},{1,17},{... | collective-permute-start | bytes 1769480 | tf_op jit(solution)/shard_map/ppermute | solution.py:566
  130.4 21.1 %collective-permute-start.23 = (bf16[64,4608]{1,0:T(8,128)(2,1)S(1)}, bf16[64,4608]{1,0:T(8,128)(2,1)S(1)}, u32[]{:S(2)}, u32[]{:S(2)}) collective-permute-start(bf16[64,4608]{1,0:T(8,128)(2,1)S(1)} %collective-permute-done.16), channel_id=1, source_target_pairs={{0,8},{4,12},{8,0},{12,4},{16,24},{20,28},{24,16},{28,20},{1,9},{5... | collective-permute-start | bytes 1769480 | tf_op jit(solution)/shard_map/ppermute | solution.py:566
  132.0 19.5 %collective-permute-start.22 = (bf16[32,4608]{1,0:T(8,128)(2,1)S(1)}, bf16[32,4608]{1,0:T(8,128)(2,1)S(1)}, u32[]{:S(2)}, u32[]{:S(2)}) collective-permute-start(bf16[32,4608]{1,0:T(8,128)(2,1)S(1)} %slice.654), channel_id=1, source_target_pairs={{0,8},{4,12},{8,0},{12,4},{16,24},{20,28},{24,16},{28,20},{1,9},{5... | collective-permute-start | bytes 884744 | tf_op jit(solution)/shard_map/ppermute | solution.py:566
  132.6 18.9 %collective-permute-start.21 = (bf16[32,4608]{1,0:T(8,128)(2,1)S(1)}, bf16[32,4608]{1,0:T(8,128)(2,1)S(1)}, u32[]{:S(2)}, u32[]{:S(2)}) collective-permute-start(bf16[32,4608]{1,0:T(8,128)(2,1)S(1)} %slice.653), channel_id=1, source_target_pairs={{0,16},{4,20},{8,24},{12,28},{16,0},{20,4},{24,8},{28,12},{1,17},{... | collective-permute-start | bytes 884744 | tf_op jit(solution)/shard_map/ppermute | solution.py:566
  136.3 14.2 %collective-permute-start.20 = (bf16[2,1,512,256]{3,2,0,1:T(8,128)(2,1)S(1)}, bf16[2,1,512,256]{3,2,0,1:T(8,128)(2,1)S(1)}, u32[]{:S(2)}, u32[]{:S(2)}) collective-permute-start(bf16[2,1,512,256]{3,2,0,1:T(8,128)(2,1)S(1)} %fusion.61), channel_id=1, source_target_pairs={{0,1},{1,0},{2,3},{3,2},{4,5},{5,4},{6,7},{7,6},{8,9},{9,8},{10,11... | collective-permute-start | bytes 1572872 | tf_op jit(solution)/shard_map/ppermute | solution.py:569
  155.1 27.2 %collective-permute-start.30 = (bf16[512,1024]{1,0:T(8,128)(2,1)S(1)}, bf16[512,1024]{1,0:T(8,128)(2,1)S(1)}, u32[]{:S(2)}, u32[]{:S(2)}) collective-permute-start(bf16[512,1024]{1,0:T(8,128)(2,1)S(1)} %copy-done.59), channel_id=1, source_target_pairs={{2,4},{3,5},{4,2},{5,3},{10,12},{11,13},{12,10},{13,11},{18,20},{1... | collective-permute-start | bytes 3145736 | tf_op jit(solution)/shard_map/ppermute | solution.py:588
  207.2 25.7 %collective-permute-start.34 = (bf16[2,2,128,1024]{3,2,0,1:T(8,128)(2,1)}, bf16[2,2,128,1024]{3,2,0,1:T(8,128)(2,1)}, u32[]{:S(2)}, u32[]{:S(2)}) collective-permute-start(bf16[2,2,128,1024]{3,2,0,1:T(8,128)(2,1)} %copy.84), channel_id=1, source_target_pairs={{0,16},{4,20},{8,24},{12,28},{16,0},{20,4},{24,8},{28,12},{1,17},{... | collective-permute-start | bytes 3145736 | tf_op jit(solution)/shard_map/ppermute | solution.py:566
  207.8 25.1 %collective-permute-start.32 = (bf16[512,1024]{1,0:T(8,128)(2,1)}, bf16[512,1024]{1,0:T(8,128)(2,1)}, u32[]{:S(2)}, u32[]{:S(2)}) collective-permute-start(bf16[512,1024]{1,0:T(8,128)(2,1)} %up_backward.3), channel_id=1, source_target_pairs={{0,4},{4,0},{8,12},{12,8},{16,20},{20,16},{24,28},{28,24},{1,5},{5... | collective-permute-start | bytes 3145736 | tf_op jit(solution)/shard_map/ppermute | solution.py:563
  207.8 25.9 %collective-permute-start.33 = (bf16[2,2,128,1024]{3,2,1,0:T(8,128)(2,1)}, bf16[2,2,128,1024]{3,2,1,0:T(8,128)(2,1)}, u32[]{:S(2)}, u32[]{:S(2)}) collective-permute-start(bf16[2,2,128,1024]{3,2,1,0:T(8,128)(2,1)} %get-tuple-element.203), channel_id=1, source_target_pairs={{0,8},{4,12},{8,0},{12,4},{16,24},{20,28},{24,16},{28,20},{1,9},{5... | collective-permute-start | bytes 3145736 | tf_op jit(solution)/shard_map/ppermute | solution.py:566
  250.0 16.0 %collective-permute-start.40 = (bf16[2,128,1024]{2,1,0:T(8,128)(2,1)S(1)}, bf16[2,128,1024]{2,1,0:T(8,128)(2,1)S(1)}, u32[]{:S(2)}, u32[]{:S(2)}) collective-permute-start(bf16[2,128,1024]{2,1,0:T(8,128)(2,1)S(1)} %dynamic-slice_bitcast_fusion.14), channel_id=1, source_target_pairs={{0,8},{4,12},{8,0},{12,4},{16,24},{20,28},{24,16},{28,20},{1,9},{5... | collective-permute-start | bytes 1572872 | tf_op jit(solution)/shard_map/ppermute | solution.py:566
  250.8 15.4 %collective-permute-start.39 = (bf16[2,128,1024]{2,1,0:T(8,128)(2,1)S(1)}, bf16[2,128,1024]{2,1,0:T(8,128)(2,1)S(1)}, u32[]{:S(2)}, u32[]{:S(2)}) collective-permute-start(bf16[2,128,1024]{2,1,0:T(8,128)(2,1)S(1)} %dynamic-slice_bitcast_fusion.15), channel_id=1, source_target_pairs={{0,16},{4,20},{8,24},{12,28},{16,0},{20,4},{24,8},{28,12},{1,17},{... | collective-permute-start | bytes 1572872 | tf_op jit(solution)/shard_map/ppermute | solution.py:566
  252.4 13.3 %collective-permute-start.38 = (bf16[2,1,512,256]{3,2,0,1:T(8,128)(2,1)S(1)}, bf16[2,1,512,256]{3,2,0,1:T(8,128)(2,1)S(1)}, u32[]{:S(2)}, u32[]{:S(2)}) collective-permute-start(bf16[2,1,512,256]{3,2,0,1:T(8,128)(2,1)S(1)} %constant_dynamic-slice_fusion.2), channel_id=1, source_target_pairs={{0,1},{1,0},{2,3},{3,2},{4,5},{5,4},{6,7},{7,6},{8,9},{9,8},{10,11... | collective-permute-start | bytes 1572872 | tf_op jit(solution)/shard_map/ppermute | solution.py:569
  252.7 42.8 %collective-permute-start.41 = (bf16[2,2,64,2048]{3,2,1,0:T(8,128)(2,1)}, bf16[2,2,64,2048]{3,2,1,0:T(8,128)(2,1)}, u32[]{:S(2)}, u32[]{:S(2)}) collective-permute-start(bf16[2,2,64,2048]{3,2,1,0:T(8,128)(2,1)} %get-tuple-element.225), channel_id=1, source_target_pairs={{0,8},{4,12},{8,0},{12,4},{16,24},{20,28},{24,16},{28,20},{1,9},{5... | collective-permute-start | bytes 3145736 | tf_op jit(solution)/shard_map/ppermute | solution.py:566
  253.5 42.0 %collective-permute-start.42 = (bf16[2,2,64,2048]{3,2,1,0:T(8,128)(2,1)}, bf16[2,2,64,2048]{3,2,1,0:T(8,128)(2,1)}, u32[]{:S(2)}, u32[]{:S(2)}) collective-permute-start(bf16[2,2,64,2048]{3,2,1,0:T(8,128)(2,1)} %get-tuple-element.226), channel_id=1, source_target_pairs={{0,16},{4,20},{8,24},{12,28},{16,0},{20,4},{24,8},{28,12},{1,17},{... | collective-permute-start | bytes 3145736 | tf_op jit(solution)/shard_map/ppermute | solution.py:566
  269.3 26.1 %collective-permute-start.44 = (bf16[2,2,64,512]{3,2,1,0:T(8,128)(2,1)}, bf16[2,2,64,512]{3,2,1,0:T(8,128)(2,1)S(1)}, u32[]{:S(2)}, u32[]{:S(2)}) collective-permute-start(bf16[2,2,64,512]{3,2,1,0:T(8,128)(2,1)} %get-tuple-element.431), channel_id=1, source_target_pairs={{0,16},{4,20},{8,24},{12,28},{16,0},{20,4},{24,8},{28,12},{1,17},{... | collective-permute-start | bytes 786440 | tf_op jit(solution)/shard_map/ppermute | solution.py:566
  270.3 25.1 %collective-permute-start.43 = (bf16[2,2,64,512]{3,2,1,0:T(8,128)(2,1)}, bf16[2,2,64,512]{3,2,1,0:T(8,128)(2,1)S(1)}, u32[]{:S(2)}, u32[]{:S(2)}) collective-permute-start(bf16[2,2,64,512]{3,2,1,0:T(8,128)(2,1)} %get-tuple-element.433), channel_id=1, source_target_pairs={{0,8},{4,12},{8,0},{12,4},{16,24},{20,28},{24,16},{28,20},{1,9},{5... | collective-permute-start | bytes 786440 | tf_op jit(solution)/shard_map/ppermute | solution.py:566
  271.4 52.6 %collective-permute-start.47 = (bf16[512,1024]{1,0:T(8,128)(2,1)}, bf16[512,1024]{1,0:T(8,128)(2,1)}, u32[]{:S(2)}, u32[]{:S(2)}) collective-permute-start(bf16[512,1024]{1,0:T(8,128)(2,1)} %add_convert_fusion.4), channel_id=1, source_target_pairs={{2,4},{3,5},{4,2},{5,3},{10,12},{11,13},{12,10},{13,11},{18,20},{1... | collective-permute-start | bytes 3145736 | tf_op jit(solution)/shard_map/ppermute | solution.py:588
  300.0 24.1 %collective-permute-start.45 = (bf16[2,64,2560]{2,1,0:T(8,128)(2,1)S(1)}, bf16[2,64,2560]{2,1,0:T(8,128)(2,1)}, u32[]{:S(2)}, u32[]{:S(2)}) collective-permute-start(bf16[2,64,2560]{2,1,0:T(8,128)(2,1)S(1)} %get-tuple-element.391), channel_id=1, source_target_pairs={{0,16},{4,20},{8,24},{12,28},{16,0},{20,4},{24,8},{28,12},{1,17},{... | collective-permute-start | bytes 1966088 | tf_op jit(solution)/shard_map/ppermute | solution.py:566
  302.2 21.9 %collective-permute-start.46 = (bf16[2,64,2560]{2,1,0:T(8,128)(2,1)S(1)}, bf16[2,64,2560]{2,1,0:T(8,128)(2,1)}, u32[]{:S(2)}, u32[]{:S(2)}) collective-permute-start(bf16[2,64,2560]{2,1,0:T(8,128)(2,1)S(1)} %get-tuple-element.389), channel_id=1, source_target_pairs={{0,8},{4,12},{8,0},{12,4},{16,24},{20,28},{24,16},{28,20},{1,9},{5... | collective-permute-start | bytes 1966088 | tf_op jit(solution)/shard_map/ppermute | solution.py:566
  336.8 17.6 %collective-permute-start.54 = (bf16[2,64,2560]{2,1,0:T(8,128)(2,1)S(1)}, bf16[2,64,2560]{2,1,0:T(8,128)(2,1)S(1)}, u32[]{:S(2)}, u32[]{:S(2)}) collective-permute-start(bf16[2,64,2560]{2,1,0:T(8,128)(2,1)S(1)} %get-tuple-element.387), channel_id=1, source_target_pairs={{0,1},{1,0},{2,3},{3,2},{4,5},{5,4},{6,7},{7,6},{8,9},{9,8},{10,11... | collective-permute-start | bytes 1966088 | tf_op jit(solution)/shard_map/ppermute | solution.py:569
  341.9 12.5 %collective-permute-start.52 = (bf16[2,64,768]{2,1,0:T(8,128)(2,1)S(1)}, bf16[2,64,768]{2,1,0:T(8,128)(2,1)S(1)}, u32[]{:S(2)}, u32[]{:S(2)}) collective-permute-start(bf16[2,64,768]{2,1,0:T(8,128)(2,1)S(1)} %get-tuple-element.437), channel_id=1, source_target_pairs={{0,16},{4,20},{8,24},{12,28},{16,0},{20,4},{24,8},{28,12},{1,17},{... | collective-permute-start | bytes 589832 | tf_op jit(solution)/shard_map/ppermute | solution.py:566
  344.5 43.1 %collective-permute-start.51 = (bf16[1,512,1024]{2,1,0:T(8,128)(2,1)S(1)}, bf16[1,512,1024]{2,1,0:T(8,128)(2,1)S(1)}, u32[]{:S(2)}, u32[]{:S(2)}) collective-permute-start(bf16[1,512,1024]{2,1,0:T(8,128)(2,1)S(1)} %fusion.53), channel_id=1, source_target_pairs={{0,1},{1,0},{2,3},{3,2},{4,5},{5,4},{6,7},{7,6},{8,9},{9,8},{10,11... | collective-permute-start | bytes 3145736 | tf_op jit(solution)/shard_map/ppermute | solution.py:569
  354.6 30.8 %collective-permute-start.56 = (bf16[1,64,2560]{2,1,0:T(8,128)(2,1)S(1)}, bf16[1,64,2560]{2,1,0:T(8,128)(2,1)S(1)}, u32[]{:S(2)}, u32[]{:S(2)}) collective-permute-start(bf16[1,64,2560]{2,1,0:T(8,128)(2,1)S(1)} %get-tuple-element.411), channel_id=1, source_target_pairs={{0,2},{1,3},{2,0},{3,1},{4,6},{5,7},{6,4},{7,5},{8,10},{9,11},{10,... | collective-permute-start | bytes 983048 | tf_op jit(solution)/shard_map/ppermute | solution.py:569
  355.4 30.1 %collective-permute-start.55 = (bf16[2,64,768]{2,1,0:T(8,128)(2,1)S(1)}, bf16[2,64,768]{2,1,0:T(8,128)(2,1)S(1)}, u32[]{:S(2)}, u32[]{:S(2)}) collective-permute-start(bf16[2,64,768]{2,1,0:T(8,128)(2,1)S(1)} %dynamic-slice_bitcast_fusion.26), channel_id=1, source_target_pairs={{0,2},{1,3},{2,0},{3,1},{4,6},{5,7},{6,4},{7,5},{8,10},{9,11},{10,... | collective-permute-start | bytes 589832 | tf_op jit(solution)/shard_map/ppermute | solution.py:569
  387.6 13.2 %collective-permute-start.59 = (bf16[128,1024]{1,0:T(8,128)(2,1)S(1)}, bf16[128,1024]{1,0:T(8,128)(2,1)S(1)}, u32[]{:S(2)}, u32[]{:S(2)}) collective-permute-start(bf16[128,1024]{1,0:T(8,128)(2,1)S(1)} %copy-done.75), channel_id=1, source_target_pairs={{0,16},{4,20},{8,24},{12,28},{16,0},{20,4},{24,8},{28,12},{1,17},{... | collective-permute-start | bytes 786440 | tf_op jit(solution)/shard_map/ppermute | solution.py:566
  388.7 12.1 %collective-permute-start.58 = (bf16[128,1024]{1,0:T(8,128)(2,1)S(1)}, bf16[128,1024]{1,0:T(8,128)(2,1)S(1)}, u32[]{:S(2)}, u32[]{:S(2)}) collective-permute-start(bf16[128,1024]{1,0:T(8,128)(2,1)S(1)} %copy-done.75), channel_id=1, source_target_pairs={{0,8},{4,12},{8,0},{12,4},{16,24},{20,28},{24,16},{28,20},{1,9},{5... | collective-permute-start | bytes 786440 | tf_op jit(solution)/shard_map/ppermute | solution.py:566
  389.8 12.7 %collective-permute-start.61 = (bf16[64,2560]{1,0:T(8,128)(2,1)S(1)}, bf16[64,2560]{1,0:T(8,128)(2,1)S(1)}, u32[]{:S(2)}, u32[]{:S(2)}) collective-permute-start(bf16[64,2560]{1,0:T(8,128)(2,1)S(1)} %fusion.103), channel_id=1, source_target_pairs={{0,16},{4,20},{8,24},{12,28},{16,0},{20,4},{24,8},{28,12},{1,17},{... | collective-permute-start | bytes 983048 | tf_op jit(solution)/shard_map/ppermute | solution.py:566
  390.8 12.5 %collective-permute-start.60 = (bf16[64,2560]{1,0:T(8,128)(2,1)S(1)}, bf16[64,2560]{1,0:T(8,128)(2,1)S(1)}, u32[]{:S(2)}, u32[]{:S(2)}) collective-permute-start(bf16[64,2560]{1,0:T(8,128)(2,1)S(1)} %fusion.103), channel_id=1, source_target_pairs={{0,8},{4,12},{8,0},{12,4},{16,24},{20,28},{24,16},{28,20},{1,9},{5... | collective-permute-start | bytes 983048 | tf_op jit(solution)/shard_map/ppermute | solution.py:566
  405.6 15.9 %collective-permute-start.72 = (bf16[64,1024]{1,0:T(8,128)(2,1)S(1)}, bf16[64,1024]{1,0:T(8,128)(2,1)S(1)}, u32[]{:S(2)}, u32[]{:S(2)}) collective-permute-start(bf16[64,1024]{1,0:T(8,128)(2,1)S(1)} %slice.791), channel_id=1, source_target_pairs={{0,8},{4,12},{8,0},{12,4},{16,24},{20,28},{24,16},{28,20},{1,9},{5... | collective-permute-start | bytes 393224 | tf_op jit(solution)/shard_map/ppermute | solution.py:566
  406.7 25.1 %collective-permute-start.67 = (bf16[512,1024]{1,0:T(8,128)(2,1)S(1)}, bf16[512,1024]{1,0:T(8,128)(2,1)}, u32[]{:S(2)}, u32[]{:S(2)}) collective-permute-start(bf16[512,1024]{1,0:T(8,128)(2,1)S(1)} %fusion.19), channel_id=1, source_target_pairs={{2,4},{3,5},{4,2},{5,3},{10,12},{11,13},{12,10},{13,11},{18,20},{1... | collective-permute-start | bytes 3145736 | tf_op jit(solution)/shard_map/ppermute | solution.py:588
  418.0 13.9 %collective-permute-start.66 = (bf16[2,256,768]{2,1,0:T(8,128)(2,1)S(1)}, bf16[2,256,768]{2,1,0:T(8,128)(2,1)}, u32[]{:S(2)}, u32[]{:S(2)}) collective-permute-start(bf16[2,256,768]{2,1,0:T(8,128)(2,1)S(1)} %bitcast.610), channel_id=1, source_target_pairs={{0,4},{4,0},{8,12},{12,8},{16,20},{20,16},{24,28},{28,24},{1,5},{5... | collective-permute-start | bytes 2359304 | tf_op jit(solution)/shard_map/ppermute | solution.py:563
  (121 other events, 973.0 us)
Sparse Core Ops, SparseCore 0:
  269.4 37.7 reduce-scatter.1
where the time goes:
time: 506 us; the launch traced here: 498 us
  waiting for transfers between devices  152 us (30%)
  Pallas kernels  111 us (22%)
  starting transfers between devices  71.7 us (14%)
  other arithmetic  55.7 us (11%)
  local copies, waits for them, and re-layouts  52.9 us (10%)
  matrix products  35.8 us (7%)
  between operations  18.9 us (4%)
    ppermute x15, waiting for transfers between devices, shard_swap(): lax.ppermute(part, 'shard', [(s, s ^ bits) for s in range(self.shards)])  108 us
    ppermute x42, starting transfers between devices, chip_swap(): lax.ppermute(part, 'rep', [(r, r ^ 2 * bits) for r in range(self.reps)])  42.7 us
    pallas_call x2, Pallas kernels, attend_backward(): pl.pallas_call(functools.partial(backward_kernel, heads, block, first_hea...  41.2 us
    ppermute x42, waiting for transfers between devices, chip_swap(): lax.ppermute(part, 'rep', [(r, r ^ 2 * bits) for r in range(self.reps)])  31.1 us
    unnamed x221, local copies, waits for them, and re-layouts  26 us
    pallas_call x1, Pallas kernels, attend_forward(): pl.pallas_call(functools.partial(forward_kernel, heads, block), grid=(blo...  22.4 us
    dot_general x3, matrix products, dot(): return jnp.dot(left_side, right_side, preferred_element_type=f32)  18.4 us
    ppermute x15, starting transfers between devices, shard_swap(): lax.ppermute(part, 'shard', [(s, s ^ bits) for s in range(self.shards)])  17.3 us
  transfers between devices with their start and end apart: 80, of which 30 were waited for; matrix products, arithmetic and copies ran while one was open for 18% of the time, Pallas kernels for 16%

commit v1 on v0

--- a/solution.py
+++ b/solution.py
@@ -1091,8 +1091,6 @@
     back_other, down_pair, up_terms, down_state = together(
         back_other, down_pair, up_terms, down_state
     )
-    up_cut = moves.reduce_cut(up_terms.reshape(shards, chips, rows_piece, up_wide), 1)
-    down_sums = moves.reduce_add(down_state)
     grad_act_two = up_backward(up_half, grad_up_pair, 0, f32) + back_other.astype(f32)
     grad_gain_two = jnp.sum(grad_act_two * normed_two, axis=0)
     grad_shift_two = jnp.sum(grad_act_two, axis=0)
@@ -1109,9 +1107,11 @@
     attn_own = jnp.where(core == 0, attn_halves[0], attn_halves[1])
     attn_other = jnp.where(core == 0, attn_halves[1], attn_halves[0])
     down_other = moves.core_swap(down_pair[row_count:])
-    grad_heads, attn_other, up_cut, down_sums, down_other = together(
-        moves.cores_exchange(to_members), moves.core_swap(attn_other), up_cut, down_sums, down_other
-    )
+    grad_heads, attn_other, up_terms, down_state, down_other = together(
+        moves.cores_exchange(to_members), moves.core_swap(attn_other), up_terms, down_state, down_other
+    )
+    up_cut = moves.reduce_cut(up_terms.reshape(shards, chips, rows_piece, up_wide), 1)
+    down_sums = moves.reduce_add(down_state)
     attn_pair = jnp.concatenate([attn_own, attn_other], axis=0)
     grad_heads = moves.members_exchange(grad_heads).reshape(group_rows, span)
     up_state = moves.reduce_start(up_cut, 1)

time: 506 us -> 508 us (level)
  waiting for transfers between devices: 152 us -> 142 us
  starting transfers between devices: 71.7 us -> 77.4 us
    ppermute x15, waiting for transfers between devices: 108 us -> 96.2 us  [shard_swap(): lax.ppermute(part, 'shard', [(s, s ^ bits) for s in range(self.shards)])]
    unnamed x221 -> x227, local copies, waits for them, and re-layouts: 26 us -> 25.2 us
  transfers between devices with their start and end apart: 80 -> 80, of which waited for: 30 -> 32; matrix products, arithmetic and copies ran while one was open for 18% -> 19% of each run, Pallas kernels for 16% -> 16%
where the time goes in v1:
time: 508 us; the launch traced here: 500 us
  waiting for transfers between devices  142 us (28%)
  Pallas kernels  110 us (22%)
  starting transfers between devices  77.4 us (15%)
  local copies, waits for them, and re-layouts  57.4 us (11%)
  other arithmetic  57.4 us (11%)
  matrix products  37.2 us (7%)
  between operations  18.8 us (4%)
    ppermute x15, waiting for transfers between devices, shard_swap(): lax.ppermute(part, 'shard', [(s, s ^ bits) for s in range(self.shards)])  96.2 us
    ppermute x42, starting transfers between devices, chip_swap(): lax.ppermute(part, 'rep', [(r, r ^ 2 * bits) for r in range(self.reps)])  42.6 us
    pallas_call x2, Pallas kernels, attend_backward(): pl.pallas_call(functools.partial(backward_kernel, heads, block, first_hea...  41.2 us
    ppermute x42, waiting for transfers between devices, chip_swap(): lax.ppermute(part, 'rep', [(r, r ^ 2 * bits) for r in range(self.reps)])  35.2 us
    unnamed x227, local copies, waits for them, and re-layouts  25.2 us
    pallas_call x1, Pallas kernels, attend_forward(): pl.pallas_call(functools.partial(forward_kernel, heads, block), grid=(blo...  22.4 us
    ppermute x15, starting transfers between devices, shard_swap(): lax.ppermute(part, 'shard', [(s, s ^ bits) for s in range(self.shards)])  19.1 us
    dot_general x3, matrix products, dot(): return jnp.dot(left_side, right_side, preferred_element_type=f32)  18.4 us
  transfers between devices with their start and end apart: 80, of which 32 were waited for; matrix products, arithmetic and copies ran while one was open for 19% of the time, Pallas kernels for 16%

profile of v1, /device:TPU:0, one launch (start us, length us, event | category | flops | bytes accessed | tf_op | source)
XLA Modules:
  0.0 499.8 jit_solution(8610257751324041932)
XLA Ops:
  10.3 2.7 collective-permute-start.1
  14.7 2.4 select_convert_fusion.1
  19.8 4.0 multiply_reduce_fusion
  31.6 2.0 copy-done.2
  35.3 10.4 %collective-permute-done.2 = bf16[64,4608]{1,0:T(8,128)(2,1)} collective-permute-done((bf16[64,4608]{1,0:T(8,128)(2,1)}, bf16[64,4608]{1,0:T(8,128)(2,1)}, u32[]{:S(2)}, u32[]{:S(2)}) %collective-permute-start.2) | collective-permute-done | bytes 589856 | tf_op jit(solution)/shard_map/ppermute | solution.py:569
  49.1 2.5 collective-permute-start.12
  56.6 17.0 %collective-permute-done.5 = bf16[2,64,768]{2,1,0:T(8,128)(2,1)S(1)} collective-permute-done((bf16[2,64,768]{2,1,0:T(8,128)(2,1)S(1)}, bf16[2,64,768]{2,1,0:T(8,128)(2,1)S(1)}, u32[]{:S(2)}, u32[]{:S(2)}) %collective-permute-start.5) | collective-permute-done | bytes 196640 | tf_op jit(solution)/shard_map/ppermute | solution.py:569
  75.9 9.0 %collective-permute-done.9 = bf16[4,64,768]{2,1,0:T(8,128)(2,1)S(1)} collective-permute-done((bf16[4,64,768]{2,1,0:T(8,128)(2,1)S(1)}, bf16[4,64,768]{2,1,0:T(8,128)(2,1)S(1)}, u32[]{:S(2)}, u32[]{:S(2)}) %collective-permute-start.9) | collective-permute-done | bytes 393248 | tf_op jit(solution)/shard_map/ppermute | solution.py:566
  86.8 9.9 %collective-permute-done.4 = bf16[1,512,1024]{2,1,0:T(8,128)(2,1)S(1)} collective-permute-done((bf16[1,512,1024]{2,1,0:T(8,128)(2,1)S(1)}, bf16[1,512,1024]{2,1,0:T(8,128)(2,1)S(1)}, u32[]{:S(2)}, u32[]{:S(2)}) %collective-permute-start.4) | collective-permute-done | bytes 1048608 | tf_op jit(solution)/shard_map/ppermute | solution.py:569
  103.4 3.9 add_convert_fusion.1.qkv_ref.refs_5_
  107.3 22.4 %attend_forward.1 = (bf16[2048,256]{1,0:T(8,128)(2,1)S(1)}, f32[8,4,256]{2,1,0:T(4,128)S(1)}) custom-call(s32[8]{0:T(128)S(1)} %get-tuple-element.168.low_ref, s32[8]{0:T(128)S(1)} %get-tuple-element.169.mid_ref, f32[4]{0:T(128)S(1)} %multiply_exponential_fusion.slope_ref.refs_2_, s32[8,1,256]{2,1,0:T(1,128)S(1)} %bitcast.585, ...), custom_call_target="tpu_custom_call" | custom-call | flops 12884901888 | bytes 5242880 | tf_op jit(solution)/shard_map/attend_forward/pallas_call | solution.py:331
  136.3 2.0 collective-permute-start.20
  138.4 12.1 %collective-permute-done.20 = bf16[2,1,512,256]{3,2,0,1:T(8,128)(2,1)S(1)} collective-permute-done((bf16[2,1,512,256]{3,2,0,1:T(8,128)(2,1)S(1)}, bf16[2,1,512,256]{3,2,0,1:T(8,128)(2,1)S(1)}, u32[]{:S(2)}, u32[]{:S(2)}) %collective-permute-start.20) | collective-permute-done | bytes 524320 | tf_op jit(solution)/shard_map/ppermute | solution.py:569
  156.0 4.8 collective-permute-done.25
  161.0 2.5 collective-permute-done.27
  166.3 2.4 collective-permute-done.28.other_ref
  168.7 13.2 %add_convert_fusion = (bf16[1024,2048]{1,0:T(8,128)(2,1)S(1)}, bf16[1024,2048]{1,0:T(8,128)(2,1)S(1)}) fusion(f32[2048]{0:T(1024)S(1)} %pad_maximum_fusion.17, bf16[1024,2048]{1,0:T(8,128)(2,1)S(1)} %bitcast.570, bf16[512,1024]{1,0:T(8,128)(2,1)S(1)} %collective-permute-done.28.other_ref, bf16[512,1024]{1,0:T(8,128)(2,1)S(1)} %add_convert_fusion.7.own_ref), kind=kOutput, calls=%fused_computation.9 | convolution fusion | flops 4353687552 | bytes 14688256 | tf_op jit(solution)/shard_map/dot_general | solution.py:54
  186.9 6.2 %convolution_convert_fusion = bf16[2048,1024]{1,0:T(8,128)(2,1)} fusion(bf16[1024,2048]{1,0:T(8,128)(2,1)S(1)} %get-tuple-element.197.hidden_ref, bf16[512,1024]{1,0:T(8,128)(2,1)S(1)} %collective-permute-done.31.other_ref, bf16[512,1024]{1,0:T(8,128)(2,1)S(1)} %get-tuple-element.329.own_ref), kind=kOutput, calls=%fused_computation.15 | convolution fusion | flops 4301258752 | bytes 10485760 | tf_op jit(solution)/shard_map/dot_general | solution.py:64
  193.1 2.7 fusion.128
  198.1 7.5 %hidden_backward.1 = (bf16[1024,2048]{1,0:T(8,128)(2,1)S(1)}, f32[1,2048]{1,0:T(1,128)S(1)}) custom-call(bf16[512,1024]{1,0:T(8,128)(2,1)S(1)} %get-tuple-element.329.own_ref, bf16[512,1024]{1,0:T(8,128)(2,1)S(1)} %collective-permute-done.31.other_ref, bf16[2048,1024]{1,0:T(8,128)(2,1)S(1)} %bitcast.573, bf16[1024,2048]{1,0:T(8,128)(2,1)S(1)} %get-tuple-element.198.slope_ref), custom_call_target="tpu_custom_call" | custom-call | flops 1 | bytes 1 | tf_op jit(solution)/shard_map/hidden_backward/pallas_call | solution.py:425
  205.6 3.1 up_backward.3
  210.4 5.1 %down_projection.1 = bf16[1024,1024]{1,0:T(8,128)(2,1)S(1)} custom-call(bf16[1024,2048]{1,0:T(8,128)(2,1)S(1)} %get-tuple-element.197.hidden_ref, bf16[2048,1024]{1,0:T(8,128)(2,1)S(1)} %bitcast.574), custom_call_target="tpu_custom_call" | custom-call | flops 1 | bytes 1 | tf_op jit(solution)/shard_map/down_projection/pallas_call | solution.py:483
  215.4 3.1 up_backward.2
  218.6 6.4 %up_gradient.1 = bf16[1024,2048]{1,0:T(8,128)(2,1)S(1)} custom-call(bf16[512,1024]{1,0:T(8,128)(2,1)S(1)} %add_convert_fusion.7.own_ref, bf16[512,1024]{1,0:T(8,128)(2,1)S(1)} %collective-permute-done.28.other_ref, bf16[1024,2048]{1,0:T(8,128)(2,1)S(1)} %get-tuple-element.199.grads_ref), custom_call_target="tpu_custom_call" | custom-call | flops 1 | bytes 1 | tf_op jit(solution)/shard_map/up_gradient/pallas_call | solution.py:520
  225.0 2.0 copy-done.7
  227.0 7.3 %collective-permute-done.34 = bf16[2,2,128,1024]{3,2,0,1:T(8,128)(2,1)S(1)} collective-permute-done((bf16[2,2,128,1024]{3,2,0,1:T(8,128)(2,1)S(1)}, bf16[2,2,128,1024]{3,2,0,1:T(8,128)(2,1)S(1)}, u32[]{:S(2)}, u32[]{:S(2)}) %collective-permute-start.34) | collective-permute-done | bytes 1048608 | tf_op jit(solution)/shard_map/ppermute | solution.py:566
  236.6 2.9 convert_reduce_fusion.2
  260.5 2.8 add_convert_fusion.4
  273.3 2.1 copy-done.29
  275.4 20.4 %attend_backward.2.refs_8_ = bf16[2048,384]{1,0:T(8,128)(2,1)S(1)} custom-call(s32[8]{0:T(128)S(1)} %get-tuple-element.220.refs_0_, s32[8]{0:T(128)S(1)} %get-tuple-element.221.refs_1_, f32[4]{0:T(128)S(1)} %multiply_exponential_fusion.slope_ref.refs_2_, s32[8,1,256]{2,1,0:T(1,128)S(1)} %bitcast.586, f32[8,4,256]{2,1,0:T(4,128)S(1)} %get-tuple-element.222.refs_4_, ...), custom_call_target="tpu_custom_call" | custom-call | flops 17179869184 | bytes 5242880 | tf_op jit(solution)/shard_map/attend_backward/pallas_call | solution.py:380
  305.0 20.9 %attend_backward.3 = bf16[2048,768]{1,0:T(8,128)(2,1)S(1)} custom-call(s32[8]{0:T(128)S(1)} %get-tuple-element.220.refs_0_, s32[8]{0:T(128)S(1)} %get-tuple-element.221.refs_1_, f32[4]{0:T(128)S(1)} %multiply_exponential_fusion.slope_ref.refs_2_, s32[8,1,256]{2,1,0:T(1,128)S(1)} %bitcast.587, f32[8,4,256]{2,1,0:T(4,128)S(1)} %get-tuple-element.222.refs_4_, ...), custom_call_target="tpu_custom_call" | custom-call | flops 17179869184 | bytes 5242880 | tf_op jit(solution)/shard_map/attend_backward/pallas_call | solution.py:380
  325.9 5.7 %convolution_convert_fusion.2 = bf16[1024,768]{1,0:T(8,128)(2,1)S(1)} fusion(bf16[2048,1024]{1,0:T(8,128)(2,1)} %bitcast.603, bf16[2048,768]{1,0:T(8,128)(2,1)S(1)} %attend_backward.3), kind=kOutput, calls=%fused_computation.90 | convolution fusion | flops 3222011904 | bytes 8912896 | tf_op jit(solution)/shard_map/dot_general | solution.py:64
  348.5 8.1 %collective-permute-done.54 = bf16[2,64,2560]{2,1,0:T(8,128)(2,1)S(1)} collective-permute-done((bf16[2,64,2560]{2,1,0:T(8,128)(2,1)S(1)}, bf16[2,64,2560]{2,1,0:T(8,128)(2,1)S(1)}, u32[]{:S(2)}, u32[]{:S(2)}) %collective-permute-start.54) | collective-permute-done | bytes 655392 | tf_op jit(solution)/shard_map/ppermute | solution.py:569
  357.8 2.2 collective-permute-start.55
  360.3 28.2 %collective-permute-done.55 = bf16[2,64,768]{2,1,0:T(8,128)(2,1)S(1)} collective-permute-done((bf16[2,64,768]{2,1,0:T(8,128)(2,1)S(1)}, bf16[2,64,768]{2,1,0:T(8,128)(2,1)S(1)}, u32[]{:S(2)}, u32[]{:S(2)}) %collective-permute-start.55) | collective-permute-done | bytes 196640 | tf_op jit(solution)/shard_map/ppermute | solution.py:569
  400.2 2.4 collective-permute-done.57
  408.1 1.9 collective-permute-start.67
  415.6 2.0 collective-permute-done.65
  424.9 2.6 collective-permute-done.71
  427.5 2.0 collective-permute-start.76
  429.6 2.1 collective-permute-done.76
  440.0 2.4 factor_stats.7
  452.1 2.3 broadcast_select_fusion.7
  456.2 3.4 collective-permute-start.78
  461.3 4.4 collective-permute-done.78
  475.7 4.2 factor_apply.4
  480.7 5.5 %factor_apply.7 = (f32[1024,1024]{1,0:T(8,128)}, f32[1024,1024]{1,0:T(8,128)}, bf16[1024,1024]{1,0:T(8,128)(2,1)}, f32[1,1024]{1,0:T(1,128)S(1)}, f32[1,128]{1,0:T(1,128)S(1)}) custom-call(bf16[1024,1024]{1,0:T(8,128)(2,1)S(1)} %pad_maximum_fusion.3.gradient_ref, f32[1024,1024]{1,0:T(8,128)S(1)} %copy-done.6, f32[1024,1]{1,0:T(8,128)S(1)} %copy-done.24, ...), custom_call_target="tpu_custom_call" | custom-call | tf_op jit(solution)/shard_map/factor_apply/pallas_call | solution.py:868
  487.0 4.2 factor_apply.6
  (635 shorter events, 181.8 us)
Async XLA Ops:
  7.2 318.7 %reduce-scatter.2.cloned.1.call-start = ((), (), s32[]{:S(2)}) async-start(), calls=%async_computation.1 | async-start | bytes 1310720 | tf_op jit(solution)/shard_map/reduce_scatter | solution.py:1134
  7.2 26.3 %collective-permute-start.3 = (s32[1,4]{1,0:T(1,128)}, s32[1,4]{1,0:T(1,128)S(1)}, u32[]{:S(2)}, u32[]{:S(2)}) collective-permute-start(s32[1,4]{1,0:T(1,128)} %param.14), channel_id=1, source_target_pairs={{0,4},{4,0},{8,12},{12,8},{16,20},{20,16},{24,28},{28,24},{1,5},{5... | collective-permute-start | bytes 56 | tf_op jit(solution)/shard_map/ppermute | solution.py:563
  10.3 24.0 %collective-permute-start.1 = (bf16[1,1,64,768]{3,2,1,0:T(8,128)(2,1)}, bf16[1,1,64,768]{3,2,1,0:T(8,128)(2,1)}, u32[]{:S(2)}, u32[]{:S(2)}) collective-permute-start(bf16[1,1,64,768]{3,2,1,0:T(8,128)(2,1)} %fusion.105), channel_id=1, source_target_pairs={{0,1},{1,0},{2,3},{3,2},{4,5},{5,4},{6,7},{7,6},{8,9},{9,8},{10,11... | collective-permute-start | bytes 294920 | tf_op jit(solution)/shard_map/ppermute | solution.py:569
  13.0 32.7 %collective-permute-start = (bf16[512,1024]{1,0:T(8,128)(2,1)}, bf16[512,1024]{1,0:T(8,128)(2,1)}, u32[]{:S(2)}, u32[]{:S(2)}) collective-permute-start(bf16[512,1024]{1,0:T(8,128)(2,1)} %param.12), channel_id=1, source_target_pairs={{2,4},{3,5},{4,2},{5,3},{10,12},{11,13},{12,10},{13,11},{18,20},{1... | collective-permute-start | bytes 3145736 | tf_op jit(solution)/shard_map/ppermute | solution.py:588
  19.8 25.9 %collective-permute-start.2 = (bf16[64,4608]{1,0:T(8,128)(2,1)}, bf16[64,4608]{1,0:T(8,128)(2,1)}, u32[]{:S(2)}, u32[]{:S(2)}) collective-permute-start(bf16[64,4608]{1,0:T(8,128)(2,1)} %pad_maximum_fusion.12), channel_id=1, source_target_pairs={{0,1},{1,0},{2,3},{3,2},{4,5},{5,4},{6,7},{7,6},{8,9},{9,8},{10,11... | collective-permute-start | bytes 1769480 | tf_op jit(solution)/shard_map/ppermute | solution.py:569
  45.7 27.9 %collective-permute-start.7 = (bf16[64,4608]{1,0:T(8,128)(2,1)}, bf16[64,4608]{1,0:T(8,128)(2,1)S(1)}, u32[]{:S(2)}, u32[]{:S(2)}) collective-permute-start(bf16[64,4608]{1,0:T(8,128)(2,1)} %collective-permute-done.2), channel_id=1, source_target_pairs={{0,16},{4,20},{8,24},{12,28},{16,0},{20,4},{24,8},{28,12},{1,17},{... | collective-permute-start | bytes 1769480 | tf_op jit(solution)/shard_map/ppermute | solution.py:566
  47.2 26.4 %collective-permute-start.6 = (bf16[64,4608]{1,0:T(8,128)(2,1)}, bf16[64,4608]{1,0:T(8,128)(2,1)S(1)}, u32[]{:S(2)}, u32[]{:S(2)}) collective-permute-start(bf16[64,4608]{1,0:T(8,128)(2,1)} %collective-permute-done.2), channel_id=1, source_target_pairs={{0,8},{4,12},{8,0},{12,4},{16,24},{20,28},{24,16},{28,20},{1,9},{5... | collective-permute-start | bytes 1769480 | tf_op jit(solution)/shard_map/ppermute | solution.py:566
  48.7 24.9 %collective-permute-start.5 = (bf16[2,64,768]{2,1,0:T(8,128)(2,1)S(1)}, bf16[2,64,768]{2,1,0:T(8,128)(2,1)S(1)}, u32[]{:S(2)}, u32[]{:S(2)}) collective-permute-start(bf16[2,64,768]{2,1,0:T(8,128)(2,1)S(1)} %maximum_bitcast_fusion.14), channel_id=1, source_target_pairs={{0,2},{1,3},{2,0},{3,1},{4,6},{5,7},{6,4},{7,5},{8,10},{9,11},{10,... | collective-permute-start | bytes 589832 | tf_op jit(solution)/shard_map/ppermute | solution.py:569
  49.1 48.6 %collective-permute-start.12 = (bf16[64,4608]{1,0:T(8,128)(2,1)}, bf16[64,4608]{1,0:T(8,128)(2,1)S(1)}, u32[]{:S(2)}, u32[]{:S(2)}) collective-permute-start(bf16[64,4608]{1,0:T(8,128)(2,1)} %pad_maximum_fusion.12), channel_id=1, source_target_pairs={{0,2},{1,3},{2,0},{3,1},{4,6},{5,7},{6,4},{7,5},{8,10},{9,11},{10,... | collective-permute-start | bytes 1769480 | tf_op jit(solution)/shard_map/ppermute | solution.py:569
  54.3 42.3 %collective-permute-start.4 = (bf16[1,512,1024]{2,1,0:T(8,128)(2,1)S(1)}, bf16[1,512,1024]{2,1,0:T(8,128)(2,1)S(1)}, u32[]{:S(2)}, u32[]{:S(2)}) collective-permute-start(bf16[1,512,1024]{2,1,0:T(8,128)(2,1)S(1)} %fusion.54), channel_id=1, source_target_pairs={{0,1},{1,0},{2,3},{3,2},{4,5},{5,4},{6,7},{7,6},{8,9},{9,8},{10,11... | collective-permute-start | bytes 3145736 | tf_op jit(solution)/shard_map/ppermute | solution.py:569
  84.9 12.7 %collective-permute-start.11 = (bf16[4,32,768]{2,1,0:T(8,128)(2,1)S(1)}, bf16[4,32,768]{2,1,0:T(8,128)(2,1)S(1)}, u32[]{:S(2)}, u32[]{:S(2)}) collective-permute-start(bf16[4,32,768]{2,1,0:T(8,128)(2,1)S(1)} %slice.828), channel_id=1, source_target_pairs={{0,8},{4,12},{8,0},{12,4},{16,24},{20,28},{24,16},{28,20},{1,9},{5... | collective-permute-start | bytes 589832 | tf_op jit(solution)/shard_map/ppermute | solution.py:566
  85.5 12.1 %collective-permute-start.10 = (bf16[4,32,768]{2,1,0:T(8,128)(2,1)S(1)}, bf16[4,32,768]{2,1,0:T(8,128)(2,1)S(1)}, u32[]{:S(2)}, u32[]{:S(2)}) collective-permute-start(bf16[4,32,768]{2,1,0:T(8,128)(2,1)S(1)} %slice.827), channel_id=1, source_target_pairs={{0,16},{4,20},{8,24},{12,28},{16,0},{20,4},{24,8},{28,12},{1,17},{... | collective-permute-start | bytes 589832 | tf_op jit(solution)/shard_map/ppermute | solution.py:566
  97.9 31.8 %collective-permute-start.18 = (bf16[32,4608]{1,0:T(8,128)(2,1)S(1)}, bf16[32,4608]{1,0:T(8,128)(2,1)S(1)}, u32[]{:S(2)}, u32[]{:S(2)}) collective-permute-start(bf16[32,4608]{1,0:T(8,128)(2,1)S(1)} %slice.652), channel_id=1, source_target_pairs={{0,8},{4,12},{8,0},{12,4},{16,24},{20,28},{24,16},{28,20},{1,9},{5... | collective-permute-start | bytes 884744 | tf_op jit(solution)/shard_map/ppermute | solution.py:566
  98.5 31.3 %collective-permute-start.17 = (bf16[32,4608]{1,0:T(8,128)(2,1)S(1)}, bf16[32,4608]{1,0:T(8,128)(2,1)S(1)}, u32[]{:S(2)}, u32[]{:S(2)}) collective-permute-start(bf16[32,4608]{1,0:T(8,128)(2,1)S(1)} %slice.651), channel_id=1, source_target_pairs={{0,16},{4,20},{8,24},{12,28},{16,0},{20,4},{24,8},{28,12},{1,17},{... | collective-permute-start | bytes 884744 | tf_op jit(solution)/shard_map/ppermute | solution.py:566
  99.2 30.6 %collective-permute-start.16 = (bf16[64,4608]{1,0:T(8,128)(2,1)S(1)}, bf16[64,4608]{1,0:T(8,128)(2,1)S(1)}, u32[]{:S(2)}, u32[]{:S(2)}) collective-permute-start(bf16[64,4608]{1,0:T(8,128)(2,1)S(1)} %collective-permute-done.12), channel_id=1, source_target_pairs={{0,1},{1,0},{2,3},{3,2},{4,5},{5,4},{6,7},{7,6},{8,9},{9,8},{10,11... | collective-permute-start | bytes 1769480 | tf_op jit(solution)/shard_map/ppermute | solution.py:569
  99.2 30.5 %collective-permute-start.15 = (bf16[64,4608]{1,0:T(8,128)(2,1)S(1)}, bf16[64,4608]{1,0:T(8,128)(2,1)S(1)}, u32[]{:S(2)}, u32[]{:S(2)}) collective-permute-start(bf16[64,4608]{1,0:T(8,128)(2,1)S(1)} %collective-permute-done.12), channel_id=1, source_target_pairs={{0,16},{4,20},{8,24},{12,28},{16,0},{20,4},{24,8},{28,12},{1,17},{... | collective-permute-start | bytes 1769480 | tf_op jit(solution)/shard_map/ppermute | solution.py:566
  101.9 27.8 %collective-permute-start.14 = (bf16[64,4608]{1,0:T(8,128)(2,1)S(1)}, bf16[64,4608]{1,0:T(8,128)(2,1)S(1)}, u32[]{:S(2)}, u32[]{:S(2)}) collective-permute-start(bf16[64,4608]{1,0:T(8,128)(2,1)S(1)} %collective-permute-done.12), channel_id=1, source_target_pairs={{0,8},{4,12},{8,0},{12,4},{16,24},{20,28},{24,16},{28,20},{1,9},{5... | collective-permute-start | bytes 1769480 | tf_op jit(solution)/shard_map/ppermute | solution.py:566
  129.9 21.7 %collective-permute-start.24 = (bf16[64,4608]{1,0:T(8,128)(2,1)S(1)}, bf16[64,4608]{1,0:T(8,128)(2,1)S(1)}, u32[]{:S(2)}, u32[]{:S(2)}) collective-permute-start(bf16[64,4608]{1,0:T(8,128)(2,1)S(1)} %collective-permute-done.16), channel_id=1, source_target_pairs={{0,16},{4,20},{8,24},{12,28},{16,0},{20,4},{24,8},{28,12},{1,17},{... | collective-permute-start | bytes 1769480 | tf_op jit(solution)/shard_map/ppermute | solution.py:566
  130.4 21.1 %collective-permute-start.23 = (bf16[64,4608]{1,0:T(8,128)(2,1)S(1)}, bf16[64,4608]{1,0:T(8,128)(2,1)S(1)}, u32[]{:S(2)}, u32[]{:S(2)}) collective-permute-start(bf16[64,4608]{1,0:T(8,128)(2,1)S(1)} %collective-permute-done.16), channel_id=1, source_target_pairs={{0,8},{4,12},{8,0},{12,4},{16,24},{20,28},{24,16},{28,20},{1,9},{5... | collective-permute-start | bytes 1769480 | tf_op jit(solution)/shard_map/ppermute | solution.py:566
  132.0 19.5 %collective-permute-start.22 = (bf16[32,4608]{1,0:T(8,128)(2,1)S(1)}, bf16[32,4608]{1,0:T(8,128)(2,1)S(1)}, u32[]{:S(2)}, u32[]{:S(2)}) collective-permute-start(bf16[32,4608]{1,0:T(8,128)(2,1)S(1)} %slice.654), channel_id=1, source_target_pairs={{0,8},{4,12},{8,0},{12,4},{16,24},{20,28},{24,16},{28,20},{1,9},{5... | collective-permute-start | bytes 884744 | tf_op jit(solution)/shard_map/ppermute | solution.py:566
  132.6 18.9 %collective-permute-start.21 = (bf16[32,4608]{1,0:T(8,128)(2,1)S(1)}, bf16[32,4608]{1,0:T(8,128)(2,1)S(1)}, u32[]{:S(2)}, u32[]{:S(2)}) collective-permute-start(bf16[32,4608]{1,0:T(8,128)(2,1)S(1)} %slice.653), channel_id=1, source_target_pairs={{0,16},{4,20},{8,24},{12,28},{16,0},{20,4},{24,8},{28,12},{1,17},{... | collective-permute-start | bytes 884744 | tf_op jit(solution)/shard_map/ppermute | solution.py:566
  136.3 14.2 %collective-permute-start.20 = (bf16[2,1,512,256]{3,2,0,1:T(8,128)(2,1)S(1)}, bf16[2,1,512,256]{3,2,0,1:T(8,128)(2,1)S(1)}, u32[]{:S(2)}, u32[]{:S(2)}) collective-permute-start(bf16[2,1,512,256]{3,2,0,1:T(8,128)(2,1)S(1)} %fusion.61), channel_id=1, source_target_pairs={{0,1},{1,0},{2,3},{3,2},{4,5},{5,4},{6,7},{7,6},{8,9},{9,8},{10,11... | collective-permute-start | bytes 1572872 | tf_op jit(solution)/shard_map/ppermute | solution.py:569
  155.1 26.7 %collective-permute-start.30 = (bf16[512,1024]{1,0:T(8,128)(2,1)S(1)}, bf16[512,1024]{1,0:T(8,128)(2,1)S(1)}, u32[]{:S(2)}, u32[]{:S(2)}) collective-permute-start(bf16[512,1024]{1,0:T(8,128)(2,1)S(1)} %copy-done.54), channel_id=1, source_target_pairs={{2,4},{3,5},{4,2},{5,3},{10,12},{11,13},{12,10},{13,11},{18,20},{1... | collective-permute-start | bytes 3145736 | tf_op jit(solution)/shard_map/ppermute | solution.py:588
  208.8 25.5 %collective-permute-start.34 = (bf16[2,2,128,1024]{3,2,0,1:T(8,128)(2,1)S(1)}, bf16[2,2,128,1024]{3,2,0,1:T(8,128)(2,1)S(1)}, u32[]{:S(2)}, u32[]{:S(2)}) collective-permute-start(bf16[2,2,128,1024]{3,2,0,1:T(8,128)(2,1)S(1)} %copy.84), channel_id=1, source_target_pairs={{0,16},{4,20},{8,24},{12,28},{16,0},{20,4},{24,8},{28,12},{1,17},{... | collective-permute-start | bytes 3145736 | tf_op jit(solution)/shard_map/ppermute | solution.py:566
  209.4 24.9 %collective-permute-start.32 = (bf16[512,1024]{1,0:T(8,128)(2,1)S(1)}, bf16[512,1024]{1,0:T(8,128)(2,1)S(1)}, u32[]{:S(2)}, u32[]{:S(2)}) collective-permute-start(bf16[512,1024]{1,0:T(8,128)(2,1)S(1)} %up_backward.3), channel_id=1, source_target_pairs={{0,4},{4,0},{8,12},{12,8},{16,20},{20,16},{24,28},{28,24},{1,5},{5... | collective-permute-start | bytes 3145736 | tf_op jit(solution)/shard_map/ppermute | solution.py:563
  209.5 25.5 %collective-permute-start.33 = (bf16[2,2,128,1024]{3,2,1,0:T(8,128)(2,1)S(1)}, bf16[2,2,128,1024]{3,2,1,0:T(8,128)(2,1)S(1)}, u32[]{:S(2)}, u32[]{:S(2)}) collective-permute-start(bf16[2,2,128,1024]{3,2,1,0:T(8,128)(2,1)S(1)} %get-tuple-element.202), channel_id=1, source_target_pairs={{0,8},{4,12},{8,0},{12,4},{16,24},{20,28},{24,16},{28,20},{1,9},{5... | collective-permute-start | bytes 3145736 | tf_op jit(solution)/shard_map/ppermute | solution.py:566
  250.3 14.2 %collective-permute-start.38 = (bf16[2,1,512,256]{3,2,0,1:T(8,128)(2,1)S(1)}, bf16[2,1,512,256]{3,2,0,1:T(8,128)(2,1)S(1)}, u32[]{:S(2)}, u32[]{:S(2)}) collective-permute-start(bf16[2,1,512,256]{3,2,0,1:T(8,128)(2,1)S(1)} %constant_dynamic-slice_fusion.2), channel_id=1, source_target_pairs={{0,1},{1,0},{2,3},{3,2},{4,5},{5,4},{6,7},{7,6},{8,9},{9,8},{10,11... | collective-permute-start | bytes 1572872 | tf_op jit(solution)/shard_map/ppermute | solution.py:569
  250.4 14.8 %collective-permute-start.39 = (bf16[2,128,1024]{2,1,0:T(8,128)(2,1)S(1)}, bf16[2,128,1024]{2,1,0:T(8,128)(2,1)S(1)}, u32[]{:S(2)}, u32[]{:S(2)}) collective-permute-start(bf16[2,128,1024]{2,1,0:T(8,128)(2,1)S(1)} %dynamic-slice_bitcast_fusion.15), channel_id=1, source_target_pairs={{0,16},{4,20},{8,24},{12,28},{16,0},{20,4},{24,8},{28,12},{1,17},{... | collective-permute-start | bytes 1572872 | tf_op jit(solution)/shard_map/ppermute | solution.py:566
  252.5 14.8 %collective-permute-start.40 = (bf16[2,128,1024]{2,1,0:T(8,128)(2,1)S(1)}, bf16[2,128,1024]{2,1,0:T(8,128)(2,1)S(1)}, u32[]{:S(2)}, u32[]{:S(2)}) collective-permute-start(bf16[2,128,1024]{2,1,0:T(8,128)(2,1)S(1)} %dynamic-slice_bitcast_fusion.14), channel_id=1, source_target_pairs={{0,8},{4,12},{8,0},{12,4},{16,24},{20,28},{24,16},{28,20},{1,9},{5... | collective-permute-start | bytes 1572872 | tf_op jit(solution)/shard_map/ppermute | solution.py:566
  257.2 38.6 %collective-permute-start.42 = (bf16[2,2,64,2048]{3,2,1,0:T(8,128)(2,1)}, bf16[2,2,64,2048]{3,2,1,0:T(8,128)(2,1)}, u32[]{:S(2)}, u32[]{:S(2)}) collective-permute-start(bf16[2,2,64,2048]{3,2,1,0:T(8,128)(2,1)} %get-tuple-element.357), channel_id=1, source_target_pairs={{0,16},{4,20},{8,24},{12,28},{16,0},{20,4},{24,8},{28,12},{1,17},{... | collective-permute-start | bytes 3145736 | tf_op jit(solution)/shard_map/ppermute | solution.py:566
  258.0 37.9 %collective-permute-start.41 = (bf16[2,2,64,2048]{3,2,1,0:T(8,128)(2,1)}, bf16[2,2,64,2048]{3,2,1,0:T(8,128)(2,1)}, u32[]{:S(2)}, u32[]{:S(2)}) collective-permute-start(bf16[2,2,64,2048]{3,2,1,0:T(8,128)(2,1)} %get-tuple-element.359), channel_id=1, source_target_pairs={{0,8},{4,12},{8,0},{12,4},{16,24},{20,28},{24,16},{28,20},{1,9},{5... | collective-permute-start | bytes 3145736 | tf_op jit(solution)/shard_map/ppermute | solution.py:566
  270.3 25.5 %collective-permute-start.44 = (bf16[2,2,64,512]{3,2,1,0:T(8,128)(2,1)}, bf16[2,2,64,512]{3,2,1,0:T(8,128)(2,1)S(1)}, u32[]{:S(2)}, u32[]{:S(2)}) collective-permute-start(bf16[2,2,64,512]{3,2,1,0:T(8,128)(2,1)} %get-tuple-element.429), channel_id=1, source_target_pairs={{0,16},{4,20},{8,24},{12,28},{16,0},{20,4},{24,8},{28,12},{1,17},{... | collective-permute-start | bytes 786440 | tf_op jit(solution)/shard_map/ppermute | solution.py:566
  270.8 25.0 %collective-permute-start.43 = (bf16[2,2,64,512]{3,2,1,0:T(8,128)(2,1)S(1)}, bf16[2,2,64,512]{3,2,1,0:T(8,128)(2,1)S(1)}, u32[]{:S(2)}, u32[]{:S(2)}) collective-permute-start(bf16[2,2,64,512]{3,2,1,0:T(8,128)(2,1)S(1)} %copy-done.72), channel_id=1, source_target_pairs={{0,8},{4,12},{8,0},{12,4},{16,24},{20,28},{24,16},{28,20},{1,9},{5... | collective-permute-start | bytes 786440 | tf_op jit(solution)/shard_map/ppermute | solution.py:566
  271.7 54.2 %collective-permute-start.47 = (bf16[512,1024]{1,0:T(8,128)(2,1)}, bf16[512,1024]{1,0:T(8,128)(2,1)}, u32[]{:S(2)}, u32[]{:S(2)}) collective-permute-start(bf16[512,1024]{1,0:T(8,128)(2,1)} %add_convert_fusion.4), channel_id=1, source_target_pairs={{2,4},{3,5},{4,2},{5,3},{10,12},{11,13},{12,10},{13,11},{18,20},{1... | collective-permute-start | bytes 3145736 | tf_op jit(solution)/shard_map/ppermute | solution.py:588
  301.3 24.6 %collective-permute-start.45 = (bf16[2,64,2560]{2,1,0:T(8,128)(2,1)S(1)}, bf16[2,64,2560]{2,1,0:T(8,128)(2,1)}, u32[]{:S(2)}, u32[]{:S(2)}) collective-permute-start(bf16[2,64,2560]{2,1,0:T(8,128)(2,1)S(1)} %get-tuple-element.389), channel_id=1, source_target_pairs={{0,16},{4,20},{8,24},{12,28},{16,0},{20,4},{24,8},{28,12},{1,17},{... | collective-permute-start | bytes 1966088 | tf_op jit(solution)/shard_map/ppermute | solution.py:566
  303.9 22.0 %collective-permute-start.46 = (bf16[2,64,2560]{2,1,0:T(8,128)(2,1)S(1)}, bf16[2,64,2560]{2,1,0:T(8,128)(2,1)}, u32[]{:S(2)}, u32[]{:S(2)}) collective-permute-start(bf16[2,64,2560]{2,1,0:T(8,128)(2,1)S(1)} %get-tuple-element.387), channel_id=1, source_target_pairs={{0,8},{4,12},{8,0},{12,4},{16,24},{20,28},{24,16},{28,20},{1,9},{5... | collective-permute-start | bytes 1966088 | tf_op jit(solution)/shard_map/ppermute | solution.py:566
  331.9 12.0 %collective-permute-start.49 = (bf16[2,2,64,768]{3,2,1,0:T(8,128)(2,1)S(1)}, bf16[2,2,64,768]{3,2,1,0:T(8,128)(2,1)S(1)}, u32[]{:S(2)}, u32[]{:S(2)}) collective-permute-start(bf16[2,2,64,768]{3,2,1,0:T(8,128)(2,1)S(1)} %get-tuple-element.405), channel_id=1, source_target_pairs={{0,16},{4,20},{8,24},{12,28},{16,0},{20,4},{24,8},{28,12},{1,17},{... | collective-permute-start | bytes 1179656 | tf_op jit(solution)/shard_map/ppermute | solution.py:566
  332.4 11.9 %collective-permute-start.48 = (bf16[2,2,64,768]{3,2,1,0:T(8,128)(2,1)S(1)}, bf16[2,2,64,768]{3,2,1,0:T(8,128)(2,1)S(1)}, u32[]{:S(2)}, u32[]{:S(2)}) collective-permute-start(bf16[2,2,64,768]{3,2,1,0:T(8,128)(2,1)S(1)} %get-tuple-element.407), channel_id=1, source_target_pairs={{0,8},{4,12},{8,0},{12,4},{16,24},{20,28},{24,16},{28,20},{1,9},{5... | collective-permute-start | bytes 1179656 | tf_op jit(solution)/shard_map/ppermute | solution.py:566
  338.9 17.7 %collective-permute-start.54 = (bf16[2,64,2560]{2,1,0:T(8,128)(2,1)S(1)}, bf16[2,64,2560]{2,1,0:T(8,128)(2,1)S(1)}, u32[]{:S(2)}, u32[]{:S(2)}) collective-permute-start(bf16[2,64,2560]{2,1,0:T(8,128)(2,1)S(1)} %get-tuple-element.385), channel_id=1, source_target_pairs={{0,1},{1,0},{2,3},{3,2},{4,5},{5,4},{6,7},{7,6},{8,9},{9,8},{10,11... | collective-permute-start | bytes 1966088 | tf_op jit(solution)/shard_map/ppermute | solution.py:569
  344.4 12.1 %collective-permute-start.52 = (bf16[2,64,768]{2,1,0:T(8,128)(2,1)S(1)}, bf16[2,64,768]{2,1,0:T(8,128)(2,1)S(1)}, u32[]{:S(2)}, u32[]{:S(2)}) collective-permute-start(bf16[2,64,768]{2,1,0:T(8,128)(2,1)S(1)} %get-tuple-element.435), channel_id=1, source_target_pairs={{0,16},{4,20},{8,24},{12,28},{16,0},{20,4},{24,8},{28,12},{1,17},{... | collective-permute-start | bytes 589832 | tf_op jit(solution)/shard_map/ppermute | solution.py:566
  347.4 42.0 %collective-permute-start.51 = (bf16[1,512,1024]{2,1,0:T(8,128)(2,1)S(1)}, bf16[1,512,1024]{2,1,0:T(8,128)(2,1)S(1)}, u32[]{:S(2)}, u32[]{:S(2)}) collective-permute-start(bf16[1,512,1024]{2,1,0:T(8,128)(2,1)S(1)} %fusion.53), channel_id=1, source_target_pairs={{0,1},{1,0},{2,3},{3,2},{4,5},{5,4},{6,7},{7,6},{8,9},{9,8},{10,11... | collective-permute-start | bytes 3145736 | tf_op jit(solution)/shard_map/ppermute | solution.py:569
  356.8 31.8 %collective-permute-start.56 = (bf16[1,64,2560]{2,1,0:T(8,128)(2,1)S(1)}, bf16[1,64,2560]{2,1,0:T(8,128)(2,1)S(1)}, u32[]{:S(2)}, u32[]{:S(2)}) collective-permute-start(bf16[1,64,2560]{2,1,0:T(8,128)(2,1)S(1)} %get-tuple-element.409), channel_id=1, source_target_pairs={{0,2},{1,3},{2,0},{3,1},{4,6},{5,7},{6,4},{7,5},{8,10},{9,11},{10,... | collective-permute-start | bytes 983048 | tf_op jit(solution)/shard_map/ppermute | solution.py:569
  357.8 30.8 %collective-permute-start.55 = (bf16[2,64,768]{2,1,0:T(8,128)(2,1)S(1)}, bf16[2,64,768]{2,1,0:T(8,128)(2,1)S(1)}, u32[]{:S(2)}, u32[]{:S(2)}) collective-permute-start(bf16[2,64,768]{2,1,0:T(8,128)(2,1)S(1)} %dynamic-slice_bitcast_fusion.26), channel_id=1, source_target_pairs={{0,2},{1,3},{2,0},{3,1},{4,6},{5,7},{6,4},{7,5},{8,10},{9,11},{10,... | collective-permute-start | bytes 589832 | tf_op jit(solution)/shard_map/ppermute | solution.py:569
  389.4 13.2 %collective-permute-start.59 = (bf16[128,1024]{1,0:T(8,128)(2,1)S(1)}, bf16[128,1024]{1,0:T(8,128)(2,1)S(1)}, u32[]{:S(2)}, u32[]{:S(2)}) collective-permute-start(bf16[128,1024]{1,0:T(8,128)(2,1)S(1)} %copy-done.73), channel_id=1, source_target_pairs={{0,16},{4,20},{8,24},{12,28},{16,0},{20,4},{24,8},{28,12},{1,17},{... | collective-permute-start | bytes 786440 | tf_op jit(solution)/shard_map/ppermute | solution.py:566
  392.6 12.6 %collective-permute-start.60 = (bf16[64,2560]{1,0:T(8,128)(2,1)S(1)}, bf16[64,2560]{1,0:T(8,128)(2,1)S(1)}, u32[]{:S(2)}, u32[]{:S(2)}) collective-permute-start(bf16[64,2560]{1,0:T(8,128)(2,1)S(1)} %fusion.103), channel_id=1, source_target_pairs={{0,8},{4,12},{8,0},{12,4},{16,24},{20,28},{24,16},{28,20},{1,9},{5... | collective-permute-start | bytes 983048 | tf_op jit(solution)/shard_map/ppermute | solution.py:566
  407.1 17.2 %collective-permute-start.72 = (bf16[64,1024]{1,0:T(8,128)(2,1)S(1)}, bf16[64,1024]{1,0:T(8,128)(2,1)S(1)}, u32[]{:S(2)}, u32[]{:S(2)}) collective-permute-start(bf16[64,1024]{1,0:T(8,128)(2,1)S(1)} %slice.791), channel_id=1, source_target_pairs={{0,8},{4,12},{8,0},{12,4},{16,24},{20,28},{24,16},{28,20},{1,9},{5... | collective-permute-start | bytes 393224 | tf_op jit(solution)/shard_map/ppermute | solution.py:566
  408.1 25.5 %collective-permute-start.67 = (bf16[512,1024]{1,0:T(8,128)(2,1)S(1)}, bf16[512,1024]{1,0:T(8,128)(2,1)}, u32[]{:S(2)}, u32[]{:S(2)}) collective-permute-start(bf16[512,1024]{1,0:T(8,128)(2,1)S(1)} %fusion.19), channel_id=1, source_target_pairs={{2,4},{3,5},{4,2},{5,3},{10,12},{11,13},{12,10},{13,11},{18,20},{1... | collective-permute-start | bytes 3145736 | tf_op jit(solution)/shard_map/ppermute | solution.py:588
  418.5 15.1 %collective-permute-start.66 = (bf16[2,256,768]{2,1,0:T(8,128)(2,1)S(1)}, bf16[2,256,768]{2,1,0:T(8,128)(2,1)}, u32[]{:S(2)}, u32[]{:S(2)}) collective-permute-start(bf16[2,256,768]{2,1,0:T(8,128)(2,1)S(1)} %bitcast.610), channel_id=1, source_target_pairs={{0,4},{4,0},{8,12},{12,8},{16,20},{20,16},{24,28},{28,24},{1,5},{5... | collective-permute-start | bytes 2359304 | tf_op jit(solution)/shard_map/ppermute | solution.py:563
  (124 other events, 1109.3 us)
Sparse Core Ops, SparseCore 0:
  270.4 38.3 reduce-scatter.1

commit v2 on v0

--- a/solution.py
+++ b/solution.py
@@ -421,7 +421,7 @@
 def hidden_backward(weight, cot_own, cot_other, slopes):
     rows, width = cot_own.shape
     breadth = slopes.shape[1]
-    tile = min(256, breadth)
+    tile = min(512, breadth)
     return pl.pallas_call(
         hidden_backward_kernel,
         grid=(breadth // tile,),
@@ -440,7 +440,7 @@
             jax.ShapeDtypeStruct((1, breadth), f32),
         ],
         compiler_params=pltpu.CompilerParams(
-            dimension_semantics=("arbitrary",), vmem_limit_bytes=12 * 1024 * 1024
+            dimension_semantics=("arbitrary",), vmem_limit_bytes=20 * 1024 * 1024
         ),
         cost_estimate=pl.CostEstimate(flops=1, bytes_accessed=1, transcendentals=0),
         name="hidden_backward",

time: 506 us -> 505 us (level)
  no operation moved by 1% of the time
where the time goes in v2:
time: 505 us; the launch traced here: 496 us
  waiting for transfers between devices  152 us (30%)
  Pallas kernels  109 us (22%)
  starting transfers between devices  71.7 us (14%)
  other arithmetic  55.7 us (11%)
  local copies, waits for them, and re-layouts  52.9 us (10%)
  matrix products  35.8 us (7%)
  between operations  18.9 us (4%)
    ppermute x15, waiting for transfers between devices, shard_swap(): lax.ppermute(part, 'shard', [(s, s ^ bits) for s in range(self.shards)])  108 us
    ppermute x42, starting transfers between devices, chip_swap(): lax.ppermute(part, 'rep', [(r, r ^ 2 * bits) for r in range(self.reps)])  42.7 us
    pallas_call x2, Pallas kernels, attend_backward(): pl.pallas_call(functools.partial(backward_kernel, heads, block, first_hea...  41.2 us
    ppermute x42, waiting for transfers between devices, chip_swap(): lax.ppermute(part, 'rep', [(r, r ^ 2 * bits) for r in range(self.reps)])  31.1 us
    unnamed x221, local copies, waits for them, and re-layouts  26 us
    pallas_call x1, Pallas kernels, attend_forward(): pl.pallas_call(functools.partial(forward_kernel, heads, block), grid=(blo...  22.4 us
    dot_general x3, matrix products, dot(): return jnp.dot(left_side, right_side, preferred_element_type=f32)  18.4 us
    ppermute x15, starting transfers between devices, shard_swap(): lax.ppermute(part, 'shard', [(s, s ^ bits) for s in range(self.shards)])  17.3 us
  transfers between devices with their start and end apart: 80, of which 30 were waited for; matrix products, arithmetic and copies ran while one was open for 18% of the time, Pallas kernels for 16%

profile of v2, /device:TPU:0, one launch (start us, length us, event | category | flops | bytes accessed | tf_op | source)
XLA Modules:
  0.0 496.5 jit_solution(14284860657825443073)
XLA Ops:
  10.3 2.7 collective-permute-start.1
  14.7 2.4 select_convert_fusion.1
  19.8 4.0 multiply_reduce_fusion
  30.9 2.0 copy-done.6
  34.6 11.0 %collective-permute-done.2 = bf16[64,4608]{1,0:T(8,128)(2,1)} collective-permute-done((bf16[64,4608]{1,0:T(8,128)(2,1)}, bf16[64,4608]{1,0:T(8,128)(2,1)}, u32[]{:S(2)}, u32[]{:S(2)}) %collective-permute-start.2) | collective-permute-done | bytes 589856 | tf_op jit(solution)/shard_map/ppermute | solution.py:569
  49.1 2.5 collective-permute-start.12
  56.6 17.0 %collective-permute-done.5 = bf16[2,64,768]{2,1,0:T(8,128)(2,1)S(1)} collective-permute-done((bf16[2,64,768]{2,1,0:T(8,128)(2,1)S(1)}, bf16[2,64,768]{2,1,0:T(8,128)(2,1)S(1)}, u32[]{:S(2)}, u32[]{:S(2)}) %collective-permute-start.5) | collective-permute-done | bytes 196640 | tf_op jit(solution)/shard_map/ppermute | solution.py:569
  75.9 9.0 %collective-permute-done.9 = bf16[4,64,768]{2,1,0:T(8,128)(2,1)S(1)} collective-permute-done((bf16[4,64,768]{2,1,0:T(8,128)(2,1)S(1)}, bf16[4,64,768]{2,1,0:T(8,128)(2,1)S(1)}, u32[]{:S(2)}, u32[]{:S(2)}) %collective-permute-start.9) | collective-permute-done | bytes 393248 | tf_op jit(solution)/shard_map/ppermute | solution.py:566
  86.8 9.9 %collective-permute-done.4 = bf16[1,512,1024]{2,1,0:T(8,128)(2,1)S(1)} collective-permute-done((bf16[1,512,1024]{2,1,0:T(8,128)(2,1)S(1)}, bf16[1,512,1024]{2,1,0:T(8,128)(2,1)S(1)}, u32[]{:S(2)}, u32[]{:S(2)}) %collective-permute-start.4) | collective-permute-done | bytes 1048608 | tf_op jit(solution)/shard_map/ppermute | solution.py:569
  103.4 3.9 add_convert_fusion.1.qkv_ref.refs_5_
  107.3 22.4 %attend_forward.1 = (bf16[2048,256]{1,0:T(8,128)(2,1)S(1)}, f32[8,4,256]{2,1,0:T(4,128)S(1)}) custom-call(s32[8]{0:T(128)S(1)} %get-tuple-element.169.low_ref, s32[8]{0:T(128)S(1)} %get-tuple-element.170.mid_ref, f32[4]{0:T(128)S(1)} %multiply_exponential_fusion.slope_ref.refs_2_, s32[8,1,256]{2,1,0:T(1,128)S(1)} %bitcast.585, ...), custom_call_target="tpu_custom_call" | custom-call | flops 12884901888 | bytes 5242880 | tf_op jit(solution)/shard_map/attend_forward/pallas_call | solution.py:331
  136.3 2.0 collective-permute-start.20
  138.4 12.1 %collective-permute-done.20 = bf16[2,1,512,256]{3,2,0,1:T(8,128)(2,1)S(1)} collective-permute-done((bf16[2,1,512,256]{3,2,0,1:T(8,128)(2,1)S(1)}, bf16[2,1,512,256]{3,2,0,1:T(8,128)(2,1)S(1)}, u32[]{:S(2)}, u32[]{:S(2)}) %collective-permute-start.20) | collective-permute-done | bytes 524320 | tf_op jit(solution)/shard_map/ppermute | solution.py:569
  156.0 4.7 collective-permute-done.25
  161.0 2.5 collective-permute-done.27
  166.8 2.4 collective-permute-done.28.other_ref
  169.2 13.1 %add_convert_fusion = (bf16[1024,2048]{1,0:T(8,128)(2,1)S(1)}, bf16[1024,2048]{1,0:T(8,128)(2,1)S(1)}) fusion(f32[2048]{0:T(1024)S(1)} %pad_maximum_fusion.17, bf16[1024,2048]{1,0:T(8,128)(2,1)S(1)} %bitcast.570, bf16[512,1024]{1,0:T(8,128)(2,1)S(1)} %collective-permute-done.28.other_ref, bf16[512,1024]{1,0:T(8,128)(2,1)S(1)} %add_convert_fusion.7.own_ref), kind=kOutput, calls=%fused_computation.9 | convolution fusion | flops 4353687552 | bytes 14688256 | tf_op jit(solution)/shard_map/dot_general | solution.py:54
  184.2 2.1 collective-permute-done.31.other_ref
  186.3 4.9 convolution_convert_fusion
  194.4 6.2 %hidden_backward.1 = (bf16[1024,2048]{1,0:T(8,128)(2,1)S(1)}, f32[1,2048]{1,0:T(1,128)S(1)}) custom-call(bf16[512,1024]{1,0:T(8,128)(2,1)S(1)} %get-tuple-element.331.own_ref, bf16[512,1024]{1,0:T(8,128)(2,1)S(1)} %collective-permute-done.31.other_ref, bf16[2048,1024]{1,0:T(8,128)(2,1)S(1)} %bitcast.573, bf16[1024,2048]{1,0:T(8,128)(2,1)S(1)} %get-tuple-element.199.slope_ref), custom_call_target="tpu_custom_call" | custom-call | flops 1 | bytes 1 | tf_op jit(solution)/shard_map/hidden_backward/pallas_call | solution.py:425
  200.6 4.2 up_backward.3
  208.7 2.2 copy-done.9
  210.9 2.2 copy-done.24
  213.1 5.0 %down_projection.1 = bf16[1024,1024]{1,0:T(8,128)(2,1)S(1)} custom-call(bf16[1024,2048]{1,0:T(8,128)(2,1)S(1)} %copy-done.24, bf16[2048,1024]{1,0:T(8,128)(2,1)S(1)} %bitcast.574), custom_call_target="tpu_custom_call" | custom-call | flops 1 | bytes 1 | tf_op jit(solution)/shard_map/down_projection/pallas_call | solution.py:483
  218.2 3.1 up_backward.2
  221.3 6.4 %up_gradient.1 = bf16[1024,2048]{1,0:T(8,128)(2,1)S(1)} custom-call(bf16[512,1024]{1,0:T(8,128)(2,1)S(1)} %add_convert_fusion.7.own_ref, bf16[512,1024]{1,0:T(8,128)(2,1)S(1)} %collective-permute-done.28.other_ref, bf16[1024,2048]{1,0:T(8,128)(2,1)S(1)} %copy-done.1), custom_call_target="tpu_custom_call" | custom-call | flops 1 | bytes 1 | tf_op jit(solution)/shard_map/up_gradient/pallas_call | solution.py:520
  227.7 3.9 collective-permute-done.34
  232.4 2.3 multiply_reduce_fusion.3
  234.7 3.7 convert_reduce_fusion.2
  255.7 8.8 %collective-permute-done.38 = bf16[2,1,512,256]{3,2,0,1:T(8,128)(2,1)S(1)} collective-permute-done((bf16[2,1,512,256]{3,2,0,1:T(8,128)(2,1)S(1)}, bf16[2,1,512,256]{3,2,0,1:T(8,128)(2,1)S(1)}, u32[]{:S(2)}, u32[]{:S(2)}) %collective-permute-start.38) | collective-permute-done | bytes 524320 | tf_op jit(solution)/shard_map/ppermute | solution.py:569
  273.7 20.4 %attend_backward.2.refs_8_ = bf16[2048,384]{1,0:T(8,128)(2,1)S(1)} custom-call(s32[8]{0:T(128)S(1)} %get-tuple-element.219.refs_0_, s32[8]{0:T(128)S(1)} %get-tuple-element.220.refs_1_, f32[4]{0:T(128)S(1)} %multiply_exponential_fusion.slope_ref.refs_2_, s32[8,1,256]{2,1,0:T(1,128)S(1)} %bitcast.586, f32[8,4,256]{2,1,0:T(4,128)S(1)} %get-tuple-element.221.refs_4_, ...), custom_call_target="tpu_custom_call" | custom-call | flops 17179869184 | bytes 5242880 | tf_op jit(solution)/shard_map/attend_backward/pallas_call | solution.py:380
  301.9 20.9 %attend_backward.3 = bf16[2048,768]{1,0:T(8,128)(2,1)S(1)} custom-call(s32[8]{0:T(128)S(1)} %get-tuple-element.219.refs_0_, s32[8]{0:T(128)S(1)} %get-tuple-element.220.refs_1_, f32[4]{0:T(128)S(1)} %multiply_exponential_fusion.slope_ref.refs_2_, s32[8,1,256]{2,1,0:T(1,128)S(1)} %bitcast.587, f32[8,4,256]{2,1,0:T(4,128)S(1)} %get-tuple-element.221.refs_4_, ...), custom_call_target="tpu_custom_call" | custom-call | flops 17179869184 | bytes 5242880 | tf_op jit(solution)/shard_map/attend_backward/pallas_call | solution.py:380
  322.9 5.7 %convolution_convert_fusion.2 = bf16[1024,768]{1,0:T(8,128)(2,1)S(1)} fusion(bf16[2048,1024]{1,0:T(8,128)(2,1)} %bitcast.603, bf16[2048,768]{1,0:T(8,128)(2,1)S(1)} %attend_backward.3), kind=kOutput, calls=%fused_computation.90 | convolution fusion | flops 3222011904 | bytes 8912896 | tf_op jit(solution)/shard_map/dot_general | solution.py:64
  344.6 8.5 %collective-permute-done.54 = bf16[2,64,2560]{2,1,0:T(8,128)(2,1)S(1)} collective-permute-done((bf16[2,64,2560]{2,1,0:T(8,128)(2,1)S(1)}, bf16[2,64,2560]{2,1,0:T(8,128)(2,1)S(1)}, u32[]{:S(2)}, u32[]{:S(2)}) %collective-permute-start.54) | collective-permute-done | bytes 655392 | tf_op jit(solution)/shard_map/ppermute | solution.py:569
  354.1 2.5 collective-permute-start.55
  356.9 27.3 %collective-permute-done.55 = bf16[2,64,768]{2,1,0:T(8,128)(2,1)S(1)} collective-permute-done((bf16[2,64,768]{2,1,0:T(8,128)(2,1)S(1)}, bf16[2,64,768]{2,1,0:T(8,128)(2,1)S(1)}, u32[]{:S(2)}, u32[]{:S(2)}) %collective-permute-start.55) | collective-permute-done | bytes 196640 | tf_op jit(solution)/shard_map/ppermute | solution.py:569
  384.2 2.2 collective-permute-done.51
  396.4 3.1 collective-permute-done.57
  412.3 3.3 collective-permute-done.65
  421.3 3.2 collective-permute-done.71
  425.7 2.9 collective-permute-done.76
  437.0 2.4 factor_stats.7
  449.7 3.5 collective-permute-done.77
  453.3 3.1 collective-permute-start.78
  458.1 4.2 collective-permute-done.78
  472.4 4.2 factor_apply.4
  477.4 5.5 %factor_apply.7 = (f32[1024,1024]{1,0:T(8,128)}, f32[1024,1024]{1,0:T(8,128)}, bf16[1024,1024]{1,0:T(8,128)(2,1)}, f32[1,1024]{1,0:T(1,128)S(1)}, f32[1,128]{1,0:T(1,128)S(1)}) custom-call(bf16[1024,1024]{1,0:T(8,128)(2,1)S(1)} %pad_maximum_fusion.3.gradient_ref, f32[1024,1024]{1,0:T(8,128)S(1)} %copy-done.12, f32[1024,1]{1,0:T(8,128)S(1)} %copy-done.31, ...), custom_call_target="tpu_custom_call" | custom-call | tf_op jit(solution)/shard_map/factor_apply/pallas_call | solution.py:868
  483.7 4.2 factor_apply.6
  (629 shorter events, 171.8 us)
Async XLA Ops:
  7.2 315.6 %reduce-scatter.2.cloned.1.call-start = ((), (), s32[]{:S(2)}) async-start(), calls=%async_computation.1 | async-start | bytes 1310720 | tf_op jit(solution)/shard_map/reduce_scatter | solution.py:1134
  7.2 25.7 %collective-permute-start.3 = (s32[1,4]{1,0:T(1,128)}, s32[1,4]{1,0:T(1,128)S(1)}, u32[]{:S(2)}, u32[]{:S(2)}) collective-permute-start(s32[1,4]{1,0:T(1,128)} %param.14), channel_id=1, source_target_pairs={{0,4},{4,0},{8,12},{12,8},{16,20},{20,16},{24,28},{28,24},{1,5},{5... | collective-permute-start | bytes 56 | tf_op jit(solution)/shard_map/ppermute | solution.py:563
  10.3 23.3 %collective-permute-start.1 = (bf16[1,1,64,768]{3,2,1,0:T(8,128)(2,1)}, bf16[1,1,64,768]{3,2,1,0:T(8,128)(2,1)}, u32[]{:S(2)}, u32[]{:S(2)}) collective-permute-start(bf16[1,1,64,768]{3,2,1,0:T(8,128)(2,1)} %fusion.105), channel_id=1, source_target_pairs={{0,1},{1,0},{2,3},{3,2},{4,5},{5,4},{6,7},{7,6},{8,9},{9,8},{10,11... | collective-permute-start | bytes 294920 | tf_op jit(solution)/shard_map/ppermute | solution.py:569
  13.0 32.6 %collective-permute-start = (bf16[512,1024]{1,0:T(8,128)(2,1)}, bf16[512,1024]{1,0:T(8,128)(2,1)}, u32[]{:S(2)}, u32[]{:S(2)}) collective-permute-start(bf16[512,1024]{1,0:T(8,128)(2,1)} %param.12), channel_id=1, source_target_pairs={{2,4},{3,5},{4,2},{5,3},{10,12},{11,13},{12,10},{13,11},{18,20},{1... | collective-permute-start | bytes 3145736 | tf_op jit(solution)/shard_map/ppermute | solution.py:588
  19.8 25.9 %collective-permute-start.2 = (bf16[64,4608]{1,0:T(8,128)(2,1)}, bf16[64,4608]{1,0:T(8,128)(2,1)}, u32[]{:S(2)}, u32[]{:S(2)}) collective-permute-start(bf16[64,4608]{1,0:T(8,128)(2,1)} %pad_maximum_fusion.12), channel_id=1, source_target_pairs={{0,1},{1,0},{2,3},{3,2},{4,5},{5,4},{6,7},{7,6},{8,9},{9,8},{10,11... | collective-permute-start | bytes 1769480 | tf_op jit(solution)/shard_map/ppermute | solution.py:569
  45.7 28.0 %collective-permute-start.7 = (bf16[64,4608]{1,0:T(8,128)(2,1)}, bf16[64,4608]{1,0:T(8,128)(2,1)S(1)}, u32[]{:S(2)}, u32[]{:S(2)}) collective-permute-start(bf16[64,4608]{1,0:T(8,128)(2,1)} %collective-permute-done.2), channel_id=1, source_target_pairs={{0,16},{4,20},{8,24},{12,28},{16,0},{20,4},{24,8},{28,12},{1,17},{... | collective-permute-start | bytes 1769480 | tf_op jit(solution)/shard_map/ppermute | solution.py:566
  47.2 26.4 %collective-permute-start.6 = (bf16[64,4608]{1,0:T(8,128)(2,1)}, bf16[64,4608]{1,0:T(8,128)(2,1)S(1)}, u32[]{:S(2)}, u32[]{:S(2)}) collective-permute-start(bf16[64,4608]{1,0:T(8,128)(2,1)} %collective-permute-done.2), channel_id=1, source_target_pairs={{0,8},{4,12},{8,0},{12,4},{16,24},{20,28},{24,16},{28,20},{1,9},{5... | collective-permute-start | bytes 1769480 | tf_op jit(solution)/shard_map/ppermute | solution.py:566
  48.7 24.9 %collective-permute-start.5 = (bf16[2,64,768]{2,1,0:T(8,128)(2,1)S(1)}, bf16[2,64,768]{2,1,0:T(8,128)(2,1)S(1)}, u32[]{:S(2)}, u32[]{:S(2)}) collective-permute-start(bf16[2,64,768]{2,1,0:T(8,128)(2,1)S(1)} %maximum_bitcast_fusion.14), channel_id=1, source_target_pairs={{0,2},{1,3},{2,0},{3,1},{4,6},{5,7},{6,4},{7,5},{8,10},{9,11},{10,... | collective-permute-start | bytes 589832 | tf_op jit(solution)/shard_map/ppermute | solution.py:569
  49.1 48.6 %collective-permute-start.12 = (bf16[64,4608]{1,0:T(8,128)(2,1)}, bf16[64,4608]{1,0:T(8,128)(2,1)S(1)}, u32[]{:S(2)}, u32[]{:S(2)}) collective-permute-start(bf16[64,4608]{1,0:T(8,128)(2,1)} %pad_maximum_fusion.12), channel_id=1, source_target_pairs={{0,2},{1,3},{2,0},{3,1},{4,6},{5,7},{6,4},{7,5},{8,10},{9,11},{10,... | collective-permute-start | bytes 1769480 | tf_op jit(solution)/shard_map/ppermute | solution.py:569
  54.3 42.3 %collective-permute-start.4 = (bf16[1,512,1024]{2,1,0:T(8,128)(2,1)S(1)}, bf16[1,512,1024]{2,1,0:T(8,128)(2,1)S(1)}, u32[]{:S(2)}, u32[]{:S(2)}) collective-permute-start(bf16[1,512,1024]{2,1,0:T(8,128)(2,1)S(1)} %fusion.54), channel_id=1, source_target_pairs={{0,1},{1,0},{2,3},{3,2},{4,5},{5,4},{6,7},{7,6},{8,9},{9,8},{10,11... | collective-permute-start | bytes 3145736 | tf_op jit(solution)/shard_map/ppermute | solution.py:569
  84.9 12.7 %collective-permute-start.11 = (bf16[4,32,768]{2,1,0:T(8,128)(2,1)S(1)}, bf16[4,32,768]{2,1,0:T(8,128)(2,1)S(1)}, u32[]{:S(2)}, u32[]{:S(2)}) collective-permute-start(bf16[4,32,768]{2,1,0:T(8,128)(2,1)S(1)} %slice.828), channel_id=1, source_target_pairs={{0,8},{4,12},{8,0},{12,4},{16,24},{20,28},{24,16},{28,20},{1,9},{5... | collective-permute-start | bytes 589832 | tf_op jit(solution)/shard_map/ppermute | solution.py:566
  85.5 12.1 %collective-permute-start.10 = (bf16[4,32,768]{2,1,0:T(8,128)(2,1)S(1)}, bf16[4,32,768]{2,1,0:T(8,128)(2,1)S(1)}, u32[]{:S(2)}, u32[]{:S(2)}) collective-permute-start(bf16[4,32,768]{2,1,0:T(8,128)(2,1)S(1)} %slice.827), channel_id=1, source_target_pairs={{0,16},{4,20},{8,24},{12,28},{16,0},{20,4},{24,8},{28,12},{1,17},{... | collective-permute-start | bytes 589832 | tf_op jit(solution)/shard_map/ppermute | solution.py:566
  97.9 31.8 %collective-permute-start.18 = (bf16[32,4608]{1,0:T(8,128)(2,1)S(1)}, bf16[32,4608]{1,0:T(8,128)(2,1)S(1)}, u32[]{:S(2)}, u32[]{:S(2)}) collective-permute-start(bf16[32,4608]{1,0:T(8,128)(2,1)S(1)} %slice.652), channel_id=1, source_target_pairs={{0,8},{4,12},{8,0},{12,4},{16,24},{20,28},{24,16},{28,20},{1,9},{5... | collective-permute-start | bytes 884744 | tf_op jit(solution)/shard_map/ppermute | solution.py:566
  98.5 31.2 %collective-permute-start.17 = (bf16[32,4608]{1,0:T(8,128)(2,1)S(1)}, bf16[32,4608]{1,0:T(8,128)(2,1)S(1)}, u32[]{:S(2)}, u32[]{:S(2)}) collective-permute-start(bf16[32,4608]{1,0:T(8,128)(2,1)S(1)} %slice.651), channel_id=1, source_target_pairs={{0,16},{4,20},{8,24},{12,28},{16,0},{20,4},{24,8},{28,12},{1,17},{... | collective-permute-start | bytes 884744 | tf_op jit(solution)/shard_map/ppermute | solution.py:566
  99.2 30.6 %collective-permute-start.16 = (bf16[64,4608]{1,0:T(8,128)(2,1)S(1)}, bf16[64,4608]{1,0:T(8,128)(2,1)S(1)}, u32[]{:S(2)}, u32[]{:S(2)}) collective-permute-start(bf16[64,4608]{1,0:T(8,128)(2,1)S(1)} %collective-permute-done.12), channel_id=1, source_target_pairs={{0,1},{1,0},{2,3},{3,2},{4,5},{5,4},{6,7},{7,6},{8,9},{9,8},{10,11... | collective-permute-start | bytes 1769480 | tf_op jit(solution)/shard_map/ppermute | solution.py:569
  99.2 30.5 %collective-permute-start.15 = (bf16[64,4608]{1,0:T(8,128)(2,1)S(1)}, bf16[64,4608]{1,0:T(8,128)(2,1)S(1)}, u32[]{:S(2)}, u32[]{:S(2)}) collective-permute-start(bf16[64,4608]{1,0:T(8,128)(2,1)S(1)} %collective-permute-done.12), channel_id=1, source_target_pairs={{0,16},{4,20},{8,24},{12,28},{16,0},{20,4},{24,8},{28,12},{1,17},{... | collective-permute-start | bytes 1769480 | tf_op jit(solution)/shard_map/ppermute | solution.py:566
  101.9 27.8 %collective-permute-start.14 = (bf16[64,4608]{1,0:T(8,128)(2,1)S(1)}, bf16[64,4608]{1,0:T(8,128)(2,1)S(1)}, u32[]{:S(2)}, u32[]{:S(2)}) collective-permute-start(bf16[64,4608]{1,0:T(8,128)(2,1)S(1)} %collective-permute-done.12), channel_id=1, source_target_pairs={{0,8},{4,12},{8,0},{12,4},{16,24},{20,28},{24,16},{28,20},{1,9},{5... | collective-permute-start | bytes 1769480 | tf_op jit(solution)/shard_map/ppermute | solution.py:566
  129.9 21.7 %collective-permute-start.24 = (bf16[64,4608]{1,0:T(8,128)(2,1)S(1)}, bf16[64,4608]{1,0:T(8,128)(2,1)S(1)}, u32[]{:S(2)}, u32[]{:S(2)}) collective-permute-start(bf16[64,4608]{1,0:T(8,128)(2,1)S(1)} %collective-permute-done.16), channel_id=1, source_target_pairs={{0,16},{4,20},{8,24},{12,28},{16,0},{20,4},{24,8},{28,12},{1,17},{... | collective-permute-start | bytes 1769480 | tf_op jit(solution)/shard_map/ppermute | solution.py:566
  130.4 21.1 %collective-permute-start.23 = (bf16[64,4608]{1,0:T(8,128)(2,1)S(1)}, bf16[64,4608]{1,0:T(8,128)(2,1)S(1)}, u32[]{:S(2)}, u32[]{:S(2)}) collective-permute-start(bf16[64,4608]{1,0:T(8,128)(2,1)S(1)} %collective-permute-done.16), channel_id=1, source_target_pairs={{0,8},{4,12},{8,0},{12,4},{16,24},{20,28},{24,16},{28,20},{1,9},{5... | collective-permute-start | bytes 1769480 | tf_op jit(solution)/shard_map/ppermute | solution.py:566
  132.0 19.5 %collective-permute-start.22 = (bf16[32,4608]{1,0:T(8,128)(2,1)S(1)}, bf16[32,4608]{1,0:T(8,128)(2,1)S(1)}, u32[]{:S(2)}, u32[]{:S(2)}) collective-permute-start(bf16[32,4608]{1,0:T(8,128)(2,1)S(1)} %slice.654), channel_id=1, source_target_pairs={{0,8},{4,12},{8,0},{12,4},{16,24},{20,28},{24,16},{28,20},{1,9},{5... | collective-permute-start | bytes 884744 | tf_op jit(solution)/shard_map/ppermute | solution.py:566
  132.6 18.9 %collective-permute-start.21 = (bf16[32,4608]{1,0:T(8,128)(2,1)S(1)}, bf16[32,4608]{1,0:T(8,128)(2,1)S(1)}, u32[]{:S(2)}, u32[]{:S(2)}) collective-permute-start(bf16[32,4608]{1,0:T(8,128)(2,1)S(1)} %slice.653), channel_id=1, source_target_pairs={{0,16},{4,20},{8,24},{12,28},{16,0},{20,4},{24,8},{28,12},{1,17},{... | collective-permute-start | bytes 884744 | tf_op jit(solution)/shard_map/ppermute | solution.py:566
  136.3 14.2 %collective-permute-start.20 = (bf16[2,1,512,256]{3,2,0,1:T(8,128)(2,1)S(1)}, bf16[2,1,512,256]{3,2,0,1:T(8,128)(2,1)S(1)}, u32[]{:S(2)}, u32[]{:S(2)}) collective-permute-start(bf16[2,1,512,256]{3,2,0,1:T(8,128)(2,1)S(1)} %fusion.61), channel_id=1, source_target_pairs={{0,1},{1,0},{2,3},{3,2},{4,5},{5,4},{6,7},{7,6},{8,9},{9,8},{10,11... | collective-permute-start | bytes 1572872 | tf_op jit(solution)/shard_map/ppermute | solution.py:569
  155.1 27.2 %collective-permute-start.30 = (bf16[512,1024]{1,0:T(8,128)(2,1)S(1)}, bf16[512,1024]{1,0:T(8,128)(2,1)S(1)}, u32[]{:S(2)}, u32[]{:S(2)}) collective-permute-start(bf16[512,1024]{1,0:T(8,128)(2,1)S(1)} %copy-done.59), channel_id=1, source_target_pairs={{2,4},{3,5},{4,2},{5,3},{10,12},{11,13},{12,10},{13,11},{18,20},{1... | collective-permute-start | bytes 3145736 | tf_op jit(solution)/shard_map/ppermute | solution.py:588
  205.9 25.8 %collective-permute-start.34 = (bf16[2,2,128,1024]{3,2,0,1:T(8,128)(2,1)}, bf16[2,2,128,1024]{3,2,0,1:T(8,128)(2,1)}, u32[]{:S(2)}, u32[]{:S(2)}) collective-permute-start(bf16[2,2,128,1024]{3,2,0,1:T(8,128)(2,1)} %copy.84), channel_id=1, source_target_pairs={{0,16},{4,20},{8,24},{12,28},{16,0},{20,4},{24,8},{28,12},{1,17},{... | collective-permute-start | bytes 3145736 | tf_op jit(solution)/shard_map/ppermute | solution.py:566
  206.5 25.1 %collective-permute-start.32 = (bf16[512,1024]{1,0:T(8,128)(2,1)}, bf16[512,1024]{1,0:T(8,128)(2,1)}, u32[]{:S(2)}, u32[]{:S(2)}) collective-permute-start(bf16[512,1024]{1,0:T(8,128)(2,1)} %up_backward.3), channel_id=1, source_target_pairs={{0,4},{4,0},{8,12},{12,8},{16,20},{20,16},{24,28},{28,24},{1,5},{5... | collective-permute-start | bytes 3145736 | tf_op jit(solution)/shard_map/ppermute | solution.py:563
  206.5 25.9 %collective-permute-start.33 = (bf16[2,2,128,1024]{3,2,1,0:T(8,128)(2,1)}, bf16[2,2,128,1024]{3,2,1,0:T(8,128)(2,1)}, u32[]{:S(2)}, u32[]{:S(2)}) collective-permute-start(bf16[2,2,128,1024]{3,2,1,0:T(8,128)(2,1)} %get-tuple-element.203), channel_id=1, source_target_pairs={{0,8},{4,12},{8,0},{12,4},{16,24},{20,28},{24,16},{28,20},{1,9},{5... | collective-permute-start | bytes 3145736 | tf_op jit(solution)/shard_map/ppermute | solution.py:566
  248.7 16.0 %collective-permute-start.40 = (bf16[2,128,1024]{2,1,0:T(8,128)(2,1)S(1)}, bf16[2,128,1024]{2,1,0:T(8,128)(2,1)S(1)}, u32[]{:S(2)}, u32[]{:S(2)}) collective-permute-start(bf16[2,128,1024]{2,1,0:T(8,128)(2,1)S(1)} %dynamic-slice_bitcast_fusion.14), channel_id=1, source_target_pairs={{0,8},{4,12},{8,0},{12,4},{16,24},{20,28},{24,16},{28,20},{1,9},{5... | collective-permute-start | bytes 1572872 | tf_op jit(solution)/shard_map/ppermute | solution.py:566
  249.6 15.4 %collective-permute-start.39 = (bf16[2,128,1024]{2,1,0:T(8,128)(2,1)S(1)}, bf16[2,128,1024]{2,1,0:T(8,128)(2,1)S(1)}, u32[]{:S(2)}, u32[]{:S(2)}) collective-permute-start(bf16[2,128,1024]{2,1,0:T(8,128)(2,1)S(1)} %dynamic-slice_bitcast_fusion.15), channel_id=1, source_target_pairs={{0,16},{4,20},{8,24},{12,28},{16,0},{20,4},{24,8},{28,12},{1,17},{... | collective-permute-start | bytes 1572872 | tf_op jit(solution)/shard_map/ppermute | solution.py:566
  251.1 13.3 %collective-permute-start.38 = (bf16[2,1,512,256]{3,2,0,1:T(8,128)(2,1)S(1)}, bf16[2,1,512,256]{3,2,0,1:T(8,128)(2,1)S(1)}, u32[]{:S(2)}, u32[]{:S(2)}) collective-permute-start(bf16[2,1,512,256]{3,2,0,1:T(8,128)(2,1)S(1)} %constant_dynamic-slice_fusion.2), channel_id=1, source_target_pairs={{0,1},{1,0},{2,3},{3,2},{4,5},{5,4},{6,7},{7,6},{8,9},{9,8},{10,11... | collective-permute-start | bytes 1572872 | tf_op jit(solution)/shard_map/ppermute | solution.py:569
  251.4 42.8 %collective-permute-start.41 = (bf16[2,2,64,2048]{3,2,1,0:T(8,128)(2,1)}, bf16[2,2,64,2048]{3,2,1,0:T(8,128)(2,1)}, u32[]{:S(2)}, u32[]{:S(2)}) collective-permute-start(bf16[2,2,64,2048]{3,2,1,0:T(8,128)(2,1)} %get-tuple-element.225), channel_id=1, source_target_pairs={{0,8},{4,12},{8,0},{12,4},{16,24},{20,28},{24,16},{28,20},{1,9},{5... | collective-permute-start | bytes 3145736 | tf_op jit(solution)/shard_map/ppermute | solution.py:566
  252.2 42.0 %collective-permute-start.42 = (bf16[2,2,64,2048]{3,2,1,0:T(8,128)(2,1)}, bf16[2,2,64,2048]{3,2,1,0:T(8,128)(2,1)}, u32[]{:S(2)}, u32[]{:S(2)}) collective-permute-start(bf16[2,2,64,2048]{3,2,1,0:T(8,128)(2,1)} %get-tuple-element.226), channel_id=1, source_target_pairs={{0,16},{4,20},{8,24},{12,28},{16,0},{20,4},{24,8},{28,12},{1,17},{... | collective-permute-start | bytes 3145736 | tf_op jit(solution)/shard_map/ppermute | solution.py:566
  268.0 26.1 %collective-permute-start.44 = (bf16[2,2,64,512]{3,2,1,0:T(8,128)(2,1)}, bf16[2,2,64,512]{3,2,1,0:T(8,128)(2,1)S(1)}, u32[]{:S(2)}, u32[]{:S(2)}) collective-permute-start(bf16[2,2,64,512]{3,2,1,0:T(8,128)(2,1)} %get-tuple-element.431), channel_id=1, source_target_pairs={{0,16},{4,20},{8,24},{12,28},{16,0},{20,4},{24,8},{28,12},{1,17},{... | collective-permute-start | bytes 786440 | tf_op jit(solution)/shard_map/ppermute | solution.py:566
  269.1 25.1 %collective-permute-start.43 = (bf16[2,2,64,512]{3,2,1,0:T(8,128)(2,1)}, bf16[2,2,64,512]{3,2,1,0:T(8,128)(2,1)S(1)}, u32[]{:S(2)}, u32[]{:S(2)}) collective-permute-start(bf16[2,2,64,512]{3,2,1,0:T(8,128)(2,1)} %get-tuple-element.433), channel_id=1, source_target_pairs={{0,8},{4,12},{8,0},{12,4},{16,24},{20,28},{24,16},{28,20},{1,9},{5... | collective-permute-start | bytes 786440 | tf_op jit(solution)/shard_map/ppermute | solution.py:566
  270.2 52.6 %collective-permute-start.47 = (bf16[512,1024]{1,0:T(8,128)(2,1)}, bf16[512,1024]{1,0:T(8,128)(2,1)}, u32[]{:S(2)}, u32[]{:S(2)}) collective-permute-start(bf16[512,1024]{1,0:T(8,128)(2,1)} %add_convert_fusion.4), channel_id=1, source_target_pairs={{2,4},{3,5},{4,2},{5,3},{10,12},{11,13},{12,10},{13,11},{18,20},{1... | collective-permute-start | bytes 3145736 | tf_op jit(solution)/shard_map/ppermute | solution.py:588
  298.7 24.1 %collective-permute-start.45 = (bf16[2,64,2560]{2,1,0:T(8,128)(2,1)S(1)}, bf16[2,64,2560]{2,1,0:T(8,128)(2,1)}, u32[]{:S(2)}, u32[]{:S(2)}) collective-permute-start(bf16[2,64,2560]{2,1,0:T(8,128)(2,1)S(1)} %get-tuple-element.391), channel_id=1, source_target_pairs={{0,16},{4,20},{8,24},{12,28},{16,0},{20,4},{24,8},{28,12},{1,17},{... | collective-permute-start | bytes 1966088 | tf_op jit(solution)/shard_map/ppermute | solution.py:566
  300.9 21.9 %collective-permute-start.46 = (bf16[2,64,2560]{2,1,0:T(8,128)(2,1)S(1)}, bf16[2,64,2560]{2,1,0:T(8,128)(2,1)}, u32[]{:S(2)}, u32[]{:S(2)}) collective-permute-start(bf16[2,64,2560]{2,1,0:T(8,128)(2,1)S(1)} %get-tuple-element.389), channel_id=1, source_target_pairs={{0,8},{4,12},{8,0},{12,4},{16,24},{20,28},{24,16},{28,20},{1,9},{5... | collective-permute-start | bytes 1966088 | tf_op jit(solution)/shard_map/ppermute | solution.py:566
  335.5 17.6 %collective-permute-start.54 = (bf16[2,64,2560]{2,1,0:T(8,128)(2,1)S(1)}, bf16[2,64,2560]{2,1,0:T(8,128)(2,1)S(1)}, u32[]{:S(2)}, u32[]{:S(2)}) collective-permute-start(bf16[2,64,2560]{2,1,0:T(8,128)(2,1)S(1)} %get-tuple-element.387), channel_id=1, source_target_pairs={{0,1},{1,0},{2,3},{3,2},{4,5},{5,4},{6,7},{7,6},{8,9},{9,8},{10,11... | collective-permute-start | bytes 1966088 | tf_op jit(solution)/shard_map/ppermute | solution.py:569
  340.6 12.5 %collective-permute-start.52 = (bf16[2,64,768]{2,1,0:T(8,128)(2,1)S(1)}, bf16[2,64,768]{2,1,0:T(8,128)(2,1)S(1)}, u32[]{:S(2)}, u32[]{:S(2)}) collective-permute-start(bf16[2,64,768]{2,1,0:T(8,128)(2,1)S(1)} %get-tuple-element.437), channel_id=1, source_target_pairs={{0,16},{4,20},{8,24},{12,28},{16,0},{20,4},{24,8},{28,12},{1,17},{... | collective-permute-start | bytes 589832 | tf_op jit(solution)/shard_map/ppermute | solution.py:566
  343.2 43.2 %collective-permute-start.51 = (bf16[1,512,1024]{2,1,0:T(8,128)(2,1)S(1)}, bf16[1,512,1024]{2,1,0:T(8,128)(2,1)S(1)}, u32[]{:S(2)}, u32[]{:S(2)}) collective-permute-start(bf16[1,512,1024]{2,1,0:T(8,128)(2,1)S(1)} %fusion.53), channel_id=1, source_target_pairs={{0,1},{1,0},{2,3},{3,2},{4,5},{5,4},{6,7},{7,6},{8,9},{9,8},{10,11... | collective-permute-start | bytes 3145736 | tf_op jit(solution)/shard_map/ppermute | solution.py:569
  353.4 30.8 %collective-permute-start.56 = (bf16[1,64,2560]{2,1,0:T(8,128)(2,1)S(1)}, bf16[1,64,2560]{2,1,0:T(8,128)(2,1)S(1)}, u32[]{:S(2)}, u32[]{:S(2)}) collective-permute-start(bf16[1,64,2560]{2,1,0:T(8,128)(2,1)S(1)} %get-tuple-element.411), channel_id=1, source_target_pairs={{0,2},{1,3},{2,0},{3,1},{4,6},{5,7},{6,4},{7,5},{8,10},{9,11},{10,... | collective-permute-start | bytes 983048 | tf_op jit(solution)/shard_map/ppermute | solution.py:569
  354.1 30.1 %collective-permute-start.55 = (bf16[2,64,768]{2,1,0:T(8,128)(2,1)S(1)}, bf16[2,64,768]{2,1,0:T(8,128)(2,1)S(1)}, u32[]{:S(2)}, u32[]{:S(2)}) collective-permute-start(bf16[2,64,768]{2,1,0:T(8,128)(2,1)S(1)} %dynamic-slice_bitcast_fusion.26), channel_id=1, source_target_pairs={{0,2},{1,3},{2,0},{3,1},{4,6},{5,7},{6,4},{7,5},{8,10},{9,11},{10,... | collective-permute-start | bytes 589832 | tf_op jit(solution)/shard_map/ppermute | solution.py:569
  386.4 13.2 %collective-permute-start.59 = (bf16[128,1024]{1,0:T(8,128)(2,1)S(1)}, bf16[128,1024]{1,0:T(8,128)(2,1)S(1)}, u32[]{:S(2)}, u32[]{:S(2)}) collective-permute-start(bf16[128,1024]{1,0:T(8,128)(2,1)S(1)} %copy-done.75), channel_id=1, source_target_pairs={{0,16},{4,20},{8,24},{12,28},{16,0},{20,4},{24,8},{28,12},{1,17},{... | collective-permute-start | bytes 786440 | tf_op jit(solution)/shard_map/ppermute | solution.py:566
  387.5 12.1 %collective-permute-start.58 = (bf16[128,1024]{1,0:T(8,128)(2,1)S(1)}, bf16[128,1024]{1,0:T(8,128)(2,1)S(1)}, u32[]{:S(2)}, u32[]{:S(2)}) collective-permute-start(bf16[128,1024]{1,0:T(8,128)(2,1)S(1)} %copy-done.75), channel_id=1, source_target_pairs={{0,8},{4,12},{8,0},{12,4},{16,24},{20,28},{24,16},{28,20},{1,9},{5... | collective-permute-start | bytes 786440 | tf_op jit(solution)/shard_map/ppermute | solution.py:566
  388.6 12.7 %collective-permute-start.61 = (bf16[64,2560]{1,0:T(8,128)(2,1)S(1)}, bf16[64,2560]{1,0:T(8,128)(2,1)S(1)}, u32[]{:S(2)}, u32[]{:S(2)}) collective-permute-start(bf16[64,2560]{1,0:T(8,128)(2,1)S(1)} %fusion.103), channel_id=1, source_target_pairs={{0,16},{4,20},{8,24},{12,28},{16,0},{20,4},{24,8},{28,12},{1,17},{... | collective-permute-start | bytes 983048 | tf_op jit(solution)/shard_map/ppermute | solution.py:566
  389.5 12.6 %collective-permute-start.60 = (bf16[64,2560]{1,0:T(8,128)(2,1)S(1)}, bf16[64,2560]{1,0:T(8,128)(2,1)S(1)}, u32[]{:S(2)}, u32[]{:S(2)}) collective-permute-start(bf16[64,2560]{1,0:T(8,128)(2,1)S(1)} %fusion.103), channel_id=1, source_target_pairs={{0,8},{4,12},{8,0},{12,4},{16,24},{20,28},{24,16},{28,20},{1,9},{5... | collective-permute-start | bytes 983048 | tf_op jit(solution)/shard_map/ppermute | solution.py:566
  404.3 16.0 %collective-permute-start.72 = (bf16[64,1024]{1,0:T(8,128)(2,1)S(1)}, bf16[64,1024]{1,0:T(8,128)(2,1)S(1)}, u32[]{:S(2)}, u32[]{:S(2)}) collective-permute-start(bf16[64,1024]{1,0:T(8,128)(2,1)S(1)} %slice.791), channel_id=1, source_target_pairs={{0,8},{4,12},{8,0},{12,4},{16,24},{20,28},{24,16},{28,20},{1,9},{5... | collective-permute-start | bytes 393224 | tf_op jit(solution)/shard_map/ppermute | solution.py:566
  405.5 25.1 %collective-permute-start.67 = (bf16[512,1024]{1,0:T(8,128)(2,1)S(1)}, bf16[512,1024]{1,0:T(8,128)(2,1)}, u32[]{:S(2)}, u32[]{:S(2)}) collective-permute-start(bf16[512,1024]{1,0:T(8,128)(2,1)S(1)} %fusion.19), channel_id=1, source_target_pairs={{2,4},{3,5},{4,2},{5,3},{10,12},{11,13},{12,10},{13,11},{18,20},{1... | collective-permute-start | bytes 3145736 | tf_op jit(solution)/shard_map/ppermute | solution.py:588
  416.7 13.9 %collective-permute-start.66 = (bf16[2,256,768]{2,1,0:T(8,128)(2,1)S(1)}, bf16[2,256,768]{2,1,0:T(8,128)(2,1)}, u32[]{:S(2)}, u32[]{:S(2)}) collective-permute-start(bf16[2,256,768]{2,1,0:T(8,128)(2,1)S(1)} %bitcast.610), channel_id=1, source_target_pairs={{0,4},{4,0},{8,12},{12,8},{16,20},{20,16},{24,28},{28,24},{1,5},{5... | collective-permute-start | bytes 2359304 | tf_op jit(solution)/shard_map/ppermute | solution.py:563
  (121 other events, 971.7 us)
Sparse Core Ops, SparseCore 0:
  268.1 37.7 reduce-scatter.1
